TPU v7x, 32 devices: a whole 2x2x4 slice. The times are simulated.
32 devices in a mesh: slab: 2 (over y), dom: 16 (over z, x, core).
Axes of the slice: x: 2, y: 2, z: 4, core: 2. Of those that a mesh axis runs over, the one named last changes fastest.
Arguments:
- state: bfloat16 [16, 64, 3072], P('dom', 'slab'), may hold values from -6 to 6
- send_index: int32 [16, 2, 16, 4], P('dom', 'slab'), may hold values from 0 to 47
- send_count: int32 [16, 2, 16], P('dom', 'slab'), may hold values from 1 to 4, as said below
- slot_target: int32 [16, 2, 64], P('dom', 'slab'), may hold values from 0 to 63
- cross_mass: bfloat16 [16, 2, 64, 4096], P('dom', 'slab'), may hold values from -0.75 to 0.75
- mass: float32 [16, 128, 4096], P('dom', 'slab'), as said below
- new_order: int32 [16, 2, 64], P('dom', 'slab'), may hold values from 0 to 63, each once within a row
Outputs:
- remapped: float32 [16, 128, 3072], P('dom', 'slab')
Inputs may be any that keep to these rules, and one draw needn't show every extreme that they name: `send_count`: each sender has exactly 4 live slots to at least one peer. Every mass block is symmetric, and each diagonal entry is positive and exceeds the sum of magnitudes of the rest of its row.
All inputs are finite; a program needn't handle non-finite values.
Results may differ from a plain program's by a relative error of at most 0.0003.
Values may be sent and summed in bfloat16 or wider, within the bound.
A program may use at most 64 MiB of HBM per device.

v0:
```python
import jax
import jax.numpy as jnp
from jax import lax
from jax.sharding import PartitionSpec as P

Q = 64
V = 48
CAP = 4
ITERS = 3
RIM = 8


def with_halo(value, sides, width):
    for axis, dim in sides:
        count, length = (lax.axis_size(axis), value.shape[dim])
        up = [(i, (i + 1) % count) for i in range(count - 1)]
        down = [(j, i) for i, j in up]
        last = lax.slice_in_dim(value, length - width, length, axis=dim)
        leading = lax.slice_in_dim(value, 0, width, axis=dim)
        before = lax.ppermute(last, axis, up)
        after = lax.ppermute(leading, axis, down)
        value = jnp.concatenate([before, value, after], axis=dim)
    return value


def apply_mass(blocks, field):
    return jnp.einsum("nqp,nvp->nvq", blocks, field, precision=lax.Precision.HIGHEST)


def local_inner(left, right):
    return jnp.sum(left * right, axis=(0, 2))[:, None]


def residual_norm(residual):
    return lax.psum(local_inner(residual, residual), ("slab", "dom"))


def solve(rhs, blocks):
    solution = jnp.zeros_like(rhs)
    residual = rhs
    direction = rhs
    norm_now = residual_norm(residual)
    for step in range(ITERS):
        image = apply_mass(blocks, direction)
        alpha = norm_now / lax.psum(local_inner(direction, image), ("slab", "dom"))
        solution = solution + alpha * direction
        residual = residual - alpha * image
        norm_next = residual_norm(residual)
        direction = residual + norm_next / norm_now * direction
        norm_now = norm_next
    return solution


def per_device(state, send_index, send_count, slot_target, cross_mass, mass, new_order):
    peers = lax.axis_size("dom")
    new_count = mass.shape[1]
    group = new_count // peers
    widened = with_halo(state, (("slab", 1),), RIM)
    candidates = widened[0]
    picks = send_index[0, 0]
    packets = jnp.take(candidates, picks.reshape(-1), axis=0).reshape(peers, CAP, V * Q)
    alive = jnp.arange(CAP)[None, :] < send_count[0, 0][:, None]
    packets = jnp.where(alive[..., None], packets, jnp.zeros_like(packets))
    received = lax.all_to_all(packets, "dom", split_axis=0, concat_axis=0, tiled=True)
    received = received.reshape(peers * CAP, V, Q)
    cross_blocks = cross_mass[0, 0].reshape(peers * CAP, Q, Q)
    contrib = jnp.einsum("jqp,jvp->jvq", cross_blocks, received, preferred_element_type=jnp.float32)
    onehot = (slot_target[0, 0][:, None] == jnp.arange(new_count)[None, :]).astype(jnp.float32)
    rhs = jnp.einsum(
        "jn,jx->nx", onehot, contrib.reshape(peers * CAP, V * Q), precision=lax.Precision.HIGHEST
    )
    order = new_order[0, 0]
    blocks = mass[0]
    solution = solve(rhs.reshape(new_count, V, Q), blocks.reshape(new_count, Q, Q))
    ordered = jnp.take(solution.reshape(new_count, V * Q), order, axis=0).reshape(
        peers, group, V * Q
    )
    moved = lax.all_to_all(ordered, "dom", split_axis=0, concat_axis=0, tiled=True)
    return moved.reshape(1, new_count, V * Q)


def solution(mesh):
    in_specs = (
        P("dom", "slab", None),
        P("dom", "slab", None, None),
        P("dom", "slab", None),
        P("dom", "slab", None),
        P("dom", "slab", None, None),
        P("dom", "slab", None),
        P("dom", "slab", None),
    )
    out_specs = P("dom", "slab", None)
    return jax.shard_map(
        per_device, mesh=mesh, in_specs=in_specs, out_specs=out_specs, check_vma=False
    )
```

profile of v0, /device:TPU:0, one launch (start us, length us, event | category | flops | bytes accessed | tf_op | source)
XLA Modules:
  0.0 292.2 jit_solution(17657374106752936908)
XLA Ops:
  0.0 0.8 fusion.13
  0.8 4.9 %collective-permute-start = (bf16[1,8,3072]{2,1,0:T(8,128)(2,1)S(1)}, bf16[1,8,3072]{2,1,0:T(8,128)(2,1)S(1)}, u32[]{:S(2)}, u32[]{:S(2)}) collective-permute-start(bf16[1,8,3072]{2,1,0:T(8,128)(2,1)S(1)} %get-tuple-element.11), channel_id=1, source_target_pairs={{0,16},{1,17},{2,18},{3,19},{4,20},{5,21},{6,22},{7,23},{8,24},{9,... | collective-permute-start | bytes 147464 | tf_op jit(solution)/shard_map/ppermute | solution.py:20
  5.7 1.3 collective-permute-start.1
  7.0 0.8 copy.24
  7.8 0.1 reshape_squeeze.12
  7.9 0.8 copy.21
  8.6 0.7 iota_compare_fusion.1
  9.4 0.0 collective-permute-done
  9.4 2.3 collective-permute-done.1
  11.7 0.9 maximum_bitcast_fusion
  12.6 0.8 gather_fusion
  13.4 0.0 copy-start.6
  13.4 0.1 gather.13
  13.6 0.0 copy-start.5
  13.6 1.1 select_select_fusion
  14.7 5.9 %all-to-all-start = ((bf16[16,4,3072]{2,1,0:T(4,128)(2,1)}), bf16[16,4,3072]{2,1,0:T(4,128)(2,1)S(1)}, u32[]{:S(2)}, u32[]{:S(2)}) async-start(bf16[16,4,3072]{2,1,0:T(4,128)(2,1)} %select_select_fusion), calls=%async_computation | async-start | bytes 786432 | tf_op jit(solution)/shard_map/all_to_all | solution.py:64
  20.6 0.0 copy-done.6
  20.7 1.1 reshape_squeeze.13
  21.8 0.0 copy-done.5
  21.8 0.0 copy-start.8
  21.8 2.2 reshape_squeeze.14
  24.0 0.5 broadcast.86
  24.5 0.0 copy-done.8
  24.5 0.6 reduce.3
  25.2 0.1 squeeze.8
  25.3 7.6 %all-to-all-done = bf16[16,4,3072]{2,1,0:T(4,128)(2,1)S(1)} async-done(((bf16[16,4,3072]{2,1,0:T(4,128)(2,1)}), bf16[16,4,3072]{2,1,0:T(4,128)(2,1)S(1)}, u32[]{:S(2)}, u32[]{:S(2)}) %all-to-all-start) | async-done | bytes 393248 | tf_op jit(solution)/shard_map/all_to_all | solution.py:64
  32.8 0.5 reshape.126
  33.3 0.7 fusion.14
  34.0 0.4 reshape.127
  34.4 0.0 copy-start.7
  34.4 0.5 copy.25
  34.9 0.2 copy-done.7
  35.1 0.0 copy-start
  35.1 2.4 fusion.8
  37.5 0.0 copy-done
  37.5 4.2 %fusion.5 = f32[64,48,64]{2,1,0:T(8,128)S(1)} fusion(f32[64,64,64]{2,1,0:T(8,128)S(1)} %copy-done, f32[64,48,64]{2,0,1:T(8,128)S(1)} %fusion.8), kind=kOutput, calls=%fused_computation.8 | convolution fusion | flops 150994944 | bytes 2621440 | tf_op jit(solution)/shard_map/nqp,nvp->nvq/dot_general | solution.py:27
  41.7 0.8 multiply_reduce_fusion.3
  42.5 38.8 %all-reduce = (f32[48,1]{0,1:T(1,128)S(1)}, f32[48,1]{0,1:T(1,128)S(1)}) all-reduce(f32[48,1]{0,1:T(1,128)S(1)} %bitcast.46, f32[48,1]{0,1:T(1,128)S(1)} %bitcast.45), channel_id=1, replica_groups=mesh['slab'=2,'dom'=16] {'slab','dom'}, use_global_device_ids=true, to_apply=%region_1.2 | all-reduce | flops 96 | bytes 768 | tf_op jit(solution)/shard_map/psum | solution.py:35
  81.3 1.8 multiply_reduce_fusion.2
  83.1 39.5 %psum.44 = f32[48,1]{0,1:T(1,128)S(1)} all-reduce(f32[48,1]{0,1:T(1,128)S(1)} %bitcast.47), channel_id=1, replica_groups=mesh['slab'=2,'dom'=16] {'slab','dom'}, use_global_device_ids=true, to_apply=%region_5.6 | all-reduce | flops 48 | bytes 384 | tf_op jit(solution)/shard_map/psum | solution.py:35
  122.6 1.8 multiply_add_fusion.2
  124.4 0.3 copy-done.1
  124.7 4.2 %fusion.3 = f32[64,48,64]{2,1,0:T(8,128)S(1)} fusion(f32[64,64,64]{2,1,0:T(8,128)S(1)} %copy-done.1, f32[64,48,64]{2,0,1:T(8,128)S(1)} %multiply_add_fusion.2), kind=kOutput, calls=%fused_computation.6 | convolution fusion | flops 150994944 | bytes 2621440 | tf_op jit(solution)/shard_map/nqp,nvp->nvq/dot_general | solution.py:27
  128.9 0.0 copy-start.3
  128.9 0.7 multiply_reduce_fusion.1
  129.7 0.4 copy-done.3
  130.1 40.4 %psum.45 = f32[48,1]{0,1:T(1,128)S(1)} all-reduce(f32[48,1]{0,1:T(1,128)S(1)} %bitcast.52), channel_id=1, replica_groups=mesh['slab'=2,'dom'=16] {'slab','dom'}, use_global_device_ids=true, to_apply=%region_7.8 | all-reduce | flops 48 | bytes 384 | tf_op jit(solution)/shard_map/psum | solution.py:45
  170.5 2.7 multiply_reduce_fusion
  173.2 39.8 %psum.46 = f32[48,1]{0,1:T(1,128)S(1)} all-reduce(f32[48,1]{0,1:T(1,128)S(1)} %bitcast.48), channel_id=1, replica_groups=mesh['slab'=2,'dom'=16] {'slab','dom'}, use_global_device_ids=true, to_apply=%region_9.10 | all-reduce | flops 48 | bytes 384 | tf_op jit(solution)/shard_map/psum | solution.py:35
  213.0 2.7 multiply_add_fusion.1
  215.7 0.0 copy-done.2
  215.7 0.0 copy-start.4
  215.7 4.2 %fusion.1 = f32[64,48,64]{2,1,0:T(8,128)S(1)} fusion(f32[64,64,64]{2,1,0:T(8,128)S(1)} %copy-done.2, f32[64,48,64]{2,0,1:T(8,128)S(1)} %multiply_add_fusion.1), kind=kOutput, calls=%fused_computation.4 | convolution fusion | flops 150994944 | bytes 2621440 | tf_op jit(solution)/shard_map/nqp,nvp->nvq/dot_general | solution.py:27
  219.9 0.0 copy-done.4
  219.9 0.8 fusion
  220.7 40.5 %psum.47 = f32[48,1]{0,1:T(1,128)S(1)} all-reduce(f32[48,1]{0,1:T(1,128)S(1)} %bitcast.51), channel_id=1, replica_groups=mesh['slab'=2,'dom'=16] {'slab','dom'}, use_global_device_ids=true, to_apply=%region_11.12 | all-reduce | flops 48 | bytes 384 | tf_op jit(solution)/shard_map/psum | solution.py:45
  261.2 1.8 multiply_add_fusion
  263.0 0.9 copy.34
  263.9 0.4 reshape.128
  264.3 0.8 gather_fusion.1
  265.2 0.2 gather.15
  265.4 0.2 broadcast_select_fusion
  265.7 25.4 %all_to_all.10 = f32[16,4,3072]{2,1,0:T(4,128)S(1)} all-to-all(f32[16,4,3072]{2,1,0:T(4,128)S(1)} %broadcast_select_fusion), channel_id=1, replica_groups=mesh['slab'=2,'dom'=16] {'dom'}, dimensions={0} | all-to-all | bytes 1572864 | tf_op jit(solution)/shard_map/all_to_all | solution.py:78
  291.1 1.1 reshape.129
  (12 shorter events, 0.0 us)
Async XLA Ops:
  0.8 8.5 %collective-permute-start = (bf16[1,8,3072]{2,1,0:T(8,128)(2,1)S(1)}, bf16[1,8,3072]{2,1,0:T(8,128)(2,1)S(1)}, u32[]{:S(2)}, u32[]{:S(2)}) collective-permute-start(bf16[1,8,3072]{2,1,0:T(8,128)(2,1)S(1)} %get-tuple-element.11), channel_id=1, source_target_pairs={{0,16},{1,17},{2,18},{3,19},{4,20},{5,21},{6,22},{7,23},{8,24},{9,... | collective-permute-start | bytes 147464 | tf_op jit(solution)/shard_map/ppermute | solution.py:20
  5.7 6.0 %collective-permute-start.1 = (bf16[1,8,3072]{2,1,0:T(8,128)(2,1)S(1)}, bf16[1,8,3072]{2,1,0:T(8,128)(2,1)S(1)}, u32[]{:S(2)}, u32[]{:S(2)}) collective-permute-start(bf16[1,8,3072]{2,1,0:T(8,128)(2,1)S(1)} %get-tuple-element.12), channel_id=1, source_target_pairs={{16,0},{17,1},{18,2},{19,3},{20,4},{21,5},{22,6},{23,7},{24,8},{25... | collective-permute-start | bytes 147464 | tf_op jit(solution)/shard_map/ppermute | solution.py:21
  13.4 7.2 %copy-start.6 = (bf16[1,1,64,4096]{3,2,1,0:T(8,128)(2,1)S(1)}, bf16[1,1,64,4096]{3,2,1,0:T(8,128)(2,1)}, u32[]{:S(2)}) copy-start(bf16[1,1,64,4096]{3,2,1,0:T(8,128)(2,1)} %param.11) | copy-start | bytes 1572868
  13.6 8.2 %copy-start.5 = (f32[1,64,4096]{2,1,0:T(8,128)S(1)}, f32[1,64,4096]{2,1,0:T(8,128)}, u32[]{:S(2)}) copy-start(f32[1,64,4096]{2,1,0:T(8,128)} %param.12) | copy-start | bytes 3145732
  14.7 18.1 %all-to-all-start = ((bf16[16,4,3072]{2,1,0:T(4,128)(2,1)}), bf16[16,4,3072]{2,1,0:T(4,128)(2,1)S(1)}, u32[]{:S(2)}, u32[]{:S(2)}) async-start(bf16[16,4,3072]{2,1,0:T(4,128)(2,1)} %select_select_fusion), calls=%async_computation | async-start | bytes 786432 | tf_op jit(solution)/shard_map/all_to_all | solution.py:64
  21.8 2.7 copy-start.8
  34.4 0.7 copy-start.7
  35.1 2.4 copy-start
  122.6 2.1 copy-start.1
  128.9 1.2 copy-start.3
  213.0 2.8 copy-start.2
  215.7 4.2 %copy-start.4 = (f32[64,48,64]{2,0,1:T(8,128)}, f32[64,48,64]{2,0,1:T(8,128)S(1)}, u32[]{:S(2)}) copy-start(f32[64,48,64]{2,0,1:T(8,128)S(1)} %multiply_add_fusion.1) | copy-start | bytes 2359300
where the time goes:
time: 294 us; the launch traced here: 292 us
  blocking collectives  224 us (76%)
  other arithmetic  16.9 us (6%)
  matrix products  15.6 us (5%)
  local copies, waits for them, and re-layouts  13.2 us (4%)
  starting transfers between devices  12.1 us (4%)
  waiting for transfers between devices  9.88 us (3%)
    psum x3, blocking collectives, residual_norm(): return lax.psum(local_inner(residual, residual), ('slab', 'dom'))  118 us
    psum x2, blocking collectives, solve(): alpha = norm_now / lax.psum(local_inner(direction, image), ('slab', 'dom'))  80.9 us
    all_to_all x1, blocking collectives, per_device(): lax.all_to_all(ordered, 'dom', split_axis=0, concat_axis=0, tiled=True)  25.4 us
    dot_general x3, matrix products, apply_mass(): jnp.einsum('nqp,nvp->nvq', blocks, field, precision=lax.Precision.HIGHEST)  12.6 us
    all_to_all x1, waiting for transfers between devices, per_device(): lax.all_to_all(packets, 'dom', split_axis=0, concat_axis=0, tiled=True)  7.57 us
    reduce_sum x5, other arithmetic, local_inner(): return jnp.sum(left * right, axis=(0, 2))[:, None]  6.84 us
    all_to_all x1, starting transfers between devices, per_device(): lax.all_to_all(packets, 'dom', split_axis=0, concat_axis=0, tiled=True)  5.91 us
  transfers between devices with their start and end apart: 3, of which 2 were waited for; matrix products, arithmetic and copies ran while one was open for 2% of the time, Pallas kernels for 0%

commit v1 on v0

v1 whole, which is shorter than its diff:
```python
import functools

import jax
import jax.numpy as jnp
from jax import lax
from jax.experimental import pallas as pl
from jax.experimental.pallas import tpu as pltpu
from jax.sharding import PartitionSpec as P

Q = 64
V = 48
RIM = 8
LANES = 128
HALF = V // 2
ITERS = 3
F32 = jnp.float32
BF16 = jnp.bfloat16
LIMIT = 32767.0


def at(index, unit):
    return pl.multiple_of(index * unit, unit)


def left_half(shape):
    return lax.broadcasted_iota(jnp.int32, shape, 1) < Q


def swap(value):
    return pltpu.roll(value, Q, 1)


def interleave(first, second):
    left = left_half(first.shape)
    return jnp.where(left, first, swap(second)), jnp.where(left, swap(first), second)


def split(value):
    high = value.astype(BF16)
    return high, (value - high.astype(F32)).astype(BF16)


def eye(rows):
    shape = (rows, LANES)
    return lax.broadcasted_iota(jnp.int32, shape, 0) == lax.broadcasted_iota(jnp.int32, shape, 1)


def column_to_row(column):
    spread = jnp.where(eye(column.shape[0]), column, 0.0)
    return jnp.sum(spread, axis=0, keepdims=True)


def row_to_column(row, rows):
    spread = jnp.where(eye(rows), row, 0.0)
    return jnp.sum(spread, axis=1, keepdims=True)


def pair_blocks(source, group, block):
    left = left_half((8, LANES))

    def body(t, carry):
        both = source[pl.ds(at(group, 16), 16), pl.ds(at(t, LANES), LANES)].astype(F32)
        first, second = both[:8], both[8:]
        block[pl.ds(2 * t, 8, stride=LANES), :] = jnp.where(left, first, 0.0)
        block[pl.ds(2 * t + 1, 8, stride=LANES), :] = jnp.where(left, swap(first), 0.0)
        block[pl.ds(Q + 2 * t, 8, stride=LANES), :] = jnp.where(left, 0.0, swap(second))
        block[pl.ds(Q + 2 * t + 1, 8, stride=LANES), :] = jnp.where(left, 0.0, second)
        return carry

    lax.fori_loop(0, Q // 2, body, 0, unroll=8)


def kernel(
    slabs, doms, cap, group,
    index_ref, count_ref, order_ref, target_ref, state_ref, cross_ref, mass_ref,
    out_ref,
    pool, up_out, down_out, up_in, down_in, packets, received, block, cross, blocks,
    contrib, residual, direction, image, answer, element, codes, codes_in, scales, scales_in,
    placed, sums, sums_in,
    halo_send, halo_recv, packet_send, packet_recv, sum_send, sum_recv,
    code_send, code_recv, scale_send, scale_recv,
):
    my_slab, my_dom = lax.axis_index("slab"), lax.axis_index("dom")
    devices = slabs * doms
    me = my_slab * doms + my_dom
    elements = state_ref.shape[0]
    slots = cross_ref.shape[0]
    new_count = mass_ref.shape[0]
    chunk = cap * HALF
    code_rows = codes.shape[0] // doms

    def device(i):
        there = lax.rem(me + i, devices)
        return {"slab": lax.div(there, doms), "dom": lax.rem(there, doms)}

    barrier = pltpu.get_barrier_semaphore()

    def greet(i, carry):
        pl.semaphore_signal(barrier, inc=1, device_id=device(i), device_id_type=pl.DeviceIdType.MESH)
        return carry

    lax.fori_loop(1, devices, greet, 0)

    def unfold(t, carry):
        for row in range(0, elements, 16):
            part = state_ref[row:row + 16, pl.ds(at(t, LANES), LANES)].astype(F32)
            pool[pl.ds((RIM + row) * HALF + t, 8, stride=HALF), :] = part[:8]
            pool[pl.ds((RIM + row + 8) * HALF + t, 8, stride=HALF), :] = part[8:]
        return carry

    lax.fori_loop(0, HALF, unfold, 0, unroll=4)
    rim_rows = RIM * HALF
    last = (RIM + elements) * HALF
    down_out[...] = pool[rim_rows:2 * rim_rows, :].astype(BF16)
    up_out[...] = pool[last - rim_rows:last, :].astype(BF16)
    pl.semaphore_wait(barrier, devices - 1)

    def halo(which, src, dst, slab):
        return pltpu.make_async_remote_copy(
            src_ref=src, dst_ref=dst, send_sem=halo_send.at[which], recv_sem=halo_recv.at[which],
            device_id={"slab": slab, "dom": my_dom}, device_id_type=pl.DeviceIdType.MESH,
        )

    up = halo(0, up_out, up_in, lax.rem(my_slab + 1, slabs))
    down = halo(1, down_out, down_in, lax.rem(my_slab + slabs - 1, slabs))

    @pl.when(my_slab < slabs - 1)
    def _():
        up.start()

    @pl.when(my_slab > 0)
    def _():
        down.start()

    def prepare_mass(j, carry):
        pair_blocks(mass_ref, j, block)

        def cut(i, inner):
            high, low = split(block[pl.ds(at(i, LANES), LANES), :])
            blocks[pl.ds(at(j * 8 + i, LANES), LANES), 0:LANES] = high
            blocks[pl.ds(at(j * 8 + i, LANES), LANES), LANES:2 * LANES] = low
            return inner

        return lax.fori_loop(0, 8, cut, carry)

    lax.fori_loop(0, new_count // 32, prepare_mass, 0)

    @pl.when(my_slab > 0)
    def _():
        up.wait_recv()
        pool[0:rim_rows, :] = up_in[...].astype(F32)

    @pl.when(my_slab == 0)
    def _():
        pool[0:rim_rows, :] = jnp.zeros((rim_rows, LANES), F32)

    @pl.when(my_slab < slabs - 1)
    def _():
        down.wait_recv()
        pool[last:last + rim_rows, :] = down_in[...].astype(F32)

    @pl.when(my_slab == slabs - 1)
    def _():
        pool[last:last + rim_rows, :] = jnp.zeros((rim_rows, LANES), F32)

    def pick(dom):
        live = count_ref[0, dom]
        rows = []
        for c in range(cap):
            row = pool[pl.ds(index_ref[dom, c] * HALF, HALF), :]
            rows.append(row * jnp.minimum(jnp.maximum(live - c, 0), 1).astype(F32))
        return jnp.concatenate(rows, axis=0).astype(BF16)

    def packet(dom):
        return pltpu.make_async_remote_copy(
            src_ref=packets.at[pl.ds(at(dom, chunk), chunk), :],
            dst_ref=received.at[pl.ds(at(my_dom, chunk), chunk), :],
            send_sem=packet_send.at[dom], recv_sem=packet_recv.at[my_dom],
            device_id={"slab": my_slab, "dom": dom}, device_id_type=pl.DeviceIdType.MESH,
        )

    def send_packet(i, carry):
        dom = lax.rem(my_dom + i, doms)
        packets[pl.ds(at(dom, chunk), chunk), :] = pick(dom)
        packet(dom).start()
        return carry

    lax.fori_loop(1, doms, send_packet, 0)
    received[pl.ds(at(my_dom, chunk), chunk), :] = pick(my_dom)

    lax.fori_loop(new_count // 32, new_count // 16, prepare_mass, 0)

    def prepare_cross(j, carry):
        pair_blocks(cross_ref, j, block)

        def cut(i, inner):
            cross[pl.ds(at(j * 8 + i, LANES), LANES), :] = block[pl.ds(at(i, LANES), LANES), :].astype(BF16)
            return inner

        return lax.fori_loop(0, 8, cut, carry)

    lax.fori_loop(0, slots // 16, prepare_cross, 0)

    def arrive(dom, carry):
        @pl.when(dom != my_dom)
        def _():
            pltpu.make_async_remote_copy(
                src_ref=packets.at[pl.ds(at(dom, chunk), chunk), :],
                dst_ref=received.at[pl.ds(at(dom, chunk), chunk), :],
                send_sem=packet_send.at[dom], recv_sem=packet_recv.at[dom],
                device_id={"slab": my_slab, "dom": dom}, device_id_type=pl.DeviceIdType.MESH,
            ).wait()

        return carry

    lax.fori_loop(0, doms, arrive, 0)

    senders = 16 // cap

    def product(step, carry):
        j, h = lax.div(step, senders // 2), lax.rem(step, senders // 2)
        first = received[pl.ds(at(j * senders + h, chunk), chunk), :].astype(F32)
        second = received[pl.ds(at(j * senders + senders // 2 + h, chunk), chunk), :].astype(F32)
        for c in range(cap):
            part = slice(c * HALF, (c + 1) * HALF)
            pair = j * 8 + h * cap + c
            field = jnp.concatenate(interleave(first[part], second[part]), axis=0).astype(BF16)
            matrix = cross[pl.ds(at(pair, LANES), LANES), :]
            contrib[pl.ds(at(pair, V), V), :] = lax.dot_general(
                field, matrix, (((1,), (1,)), ((), ())), preferred_element_type=F32
            )
        return carry

    lax.fori_loop(0, doms // 2, product, 0)

    shape = (new_count, slots)
    onehot = jnp.where(lax.broadcasted_iota(jnp.int32, shape, 0) == target_ref[...], 1.0, 0.0).astype(BF16)
    pairs_in = slots // 2

    def scatter(t, carry):
        even = contrib[pl.ds(t, pairs_in, stride=V), :]
        odd = contrib[pl.ds(HALF + t, pairs_in, stride=V), :]
        first, second = interleave(even, odd)
        rows = []
        for j in range(pairs_in // 8):
            rows += [first[j * 8:j * 8 + 8], second[j * 8:j * 8 + 8]]
        terms = jnp.concatenate(split(jnp.concatenate(rows, axis=0)), axis=1)
        total = jnp.dot(onehot, terms, preferred_element_type=F32)
        total = total[:, :LANES] + total[:, LANES:]
        for j in range(new_count // 16):
            even, odd = interleave(total[j * 16:j * 16 + 8], total[j * 16 + 8:j * 16 + 16])
            residual[pl.ds(j * 8 * V + t, 8, stride=V), :] = even
            residual[pl.ds(j * 8 * V + HALF + t, 8, stride=V), :] = odd
        return carry

    lax.fori_loop(0, HALF, scatter, 0, unroll=2)

    pairs = new_count // 2

    def apply_mass(pair, field):
        terms = jnp.concatenate(split(field), axis=0)
        result = jnp.dot(terms, blocks[pl.ds(at(pair, LANES), LANES), :], preferred_element_type=F32)
        return (result[V:, :LANES] + result[:V, LANES:]) + result[:V, :LANES]

    def all_sum(step, left, right):
        own = column_to_row(jnp.sum(jnp.concatenate([left, right], axis=0), axis=1, keepdims=True))
        sums[step:step + 1, :] = own

        def send(i, carry):
            pltpu.make_async_remote_copy(
                src_ref=sums.at[step:step + 1, :],
                dst_ref=sums_in.at[step, pl.ds(i - 1, 1), :],
                send_sem=sum_send.at[step, i - 1], recv_sem=sum_recv.at[step, i - 1],
                device_id=device(i), device_id_type=pl.DeviceIdType.MESH,
            ).start()
            return carry

        def wait(i, carry):
            pltpu.make_async_remote_copy(
                src_ref=sums.at[step:step + 1, :],
                dst_ref=sums_in.at[step, pl.ds(i - 1, 1), :],
                send_sem=sum_send.at[step, i - 1], recv_sem=sum_recv.at[step, i - 1],
                device_id=device(i), device_id_type=pl.DeviceIdType.MESH,
            ).wait()
            return carry

        lax.fori_loop(1, devices, send, 0)
        lax.fori_loop(1, devices, wait, 0)
        total = own + jnp.sum(sums_in[step, 0:devices - 1, :], axis=0, keepdims=True)
        column = row_to_column(total, 2 * V)
        return column[:V], column[V:]

    zero = jnp.zeros((V, LANES), F32)

    def first_pass(pair, carry):
        rr, rw = carry
        at_pair = pl.ds(at(pair, V), V)
        r = residual[at_pair, :]
        w = apply_mass(pair, r)
        image[at_pair, :] = w
        return rr + r * r, rw + r * w

    rr, rw = all_sum(0, *lax.fori_loop(0, pairs, first_pass, (zero, zero), unroll=2))
    alpha = rr / rw

    def second_pass(pair, carry):
        nn, nw = carry
        at_pair = pl.ds(at(pair, V), V)
        p = residual[at_pair, :]
        r = p - alpha * image[at_pair, :]
        direction[at_pair, :] = p
        answer[at_pair, :] = alpha * p
        residual[at_pair, :] = r
        w = apply_mass(pair, r)
        contrib_w[at_pair, :] = w
        return nn + r * r, nw + r * w

    contrib_w = element
    nn, nw = all_sum(1, *lax.fori_loop(0, pairs, second_pass, (zero, zero), unroll=2))
    beta = nn / rr
    alpha = nn / (nw - beta * nn / alpha)
    rr = nn

    def third_pass(pair, carry):
        nn, nw = carry
        at_pair = pl.ds(at(pair, V), V)
        r = residual[at_pair, :]
        p = r + beta * direction[at_pair, :]
        s = contrib_w[at_pair, :] + beta * image[at_pair, :]
        direction[at_pair, :] = p
        answer[at_pair, :] = answer[at_pair, :] + alpha * p
        r = r - alpha * s
        residual[at_pair, :] = r
        w = apply_mass(pair, r)
        return nn + r * r, nw + r * w

    nn, nw = all_sum(2, *lax.fori_loop(0, pairs, third_pass, (zero, zero), unroll=2))
    beta = nn / rr
    alpha = nn / (nw - beta * nn / alpha)

    def last_pass(pair, carry):
        at_pair = pl.ds(at(pair, V), V)
        p = residual[at_pair, :] + beta * direction[at_pair, :]
        x = answer[at_pair, :] + alpha * p
        first, second = interleave(x[:HALF], x[HALF:])
        number = lax.div(pair, 8) * 16 + lax.rem(pair, 8)
        element[pl.ds(at(number, HALF), HALF), :] = first
        element[pl.ds(at(number + 8, HALF), HALF), :] = second
        return carry

    lax.fori_loop(0, pairs, last_pass, 0, unroll=2)

    used = group * HALF

    def code(dom):
        rows = [
            element[pl.ds(order_ref[0, dom * group + g] * HALF, HALF), :] for g in range(group)
        ]
        value = jnp.concatenate(rows, axis=0)
        top = jnp.maximum(jnp.max(jnp.abs(value), axis=1, keepdims=True), 1e-30)
        coded = jnp.round(value * (LIMIT / top)).astype(jnp.int32)
        if code_rows > used:
            coded = jnp.concatenate([coded, jnp.zeros((code_rows - used, LANES), jnp.int32)], axis=0)
        return coded.astype(jnp.int16), column_to_row(top * (1.0 / LIMIT))

    def code_copies(to, frm, dst):
        where = {"slab": my_slab, "dom": to}
        return [
            pltpu.make_async_remote_copy(
                src_ref=codes.at[pl.ds(at(to, code_rows), code_rows), :],
                dst_ref=codes_in.at[pl.ds(at(dst, code_rows), code_rows), :],
                send_sem=code_send.at[to], recv_sem=code_recv.at[frm],
                device_id=where, device_id_type=pl.DeviceIdType.MESH,
            ),
            pltpu.make_async_remote_copy(
                src_ref=scales.at[pl.ds(to, 1), :], dst_ref=scales_in.at[pl.ds(dst, 1), :],
                send_sem=scale_send.at[to], recv_sem=scale_recv.at[frm],
                device_id=where, device_id_type=pl.DeviceIdType.MESH,
            ),
        ]

    def send_code(i, carry):
        dom = lax.rem(my_dom + i, doms)
        coded, scale = code(dom)
        codes[pl.ds(at(dom, code_rows), code_rows), :] = coded
        scales[pl.ds(dom, 1), :] = scale
        for copy in code_copies(dom, my_dom, my_dom):
            copy.start()
        return carry

    lax.fori_loop(1, doms, send_code, 0)
    coded, scale = code(my_dom)
    codes_in[pl.ds(at(my_dom, code_rows), code_rows), :] = coded
    scales_in[pl.ds(my_dom, 1), :] = scale

    def place(dom, carry):
        @pl.when(dom != my_dom)
        def _():
            for copy in code_copies(dom, dom, dom):
                copy.wait()

        value = codes_in[pl.ds(at(dom, code_rows), code_rows), :].astype(jnp.int32).astype(F32)[:used]
        scale = row_to_column(scales_in[pl.ds(dom, 1), :], used)
        placed[pl.ds(at(dom, used), used), :] = value * scale
        return carry

    lax.fori_loop(0, doms, place, 0)

    def fold(t, carry):
        for row in range(0, new_count, 8):
            out_ref[row:row + 8, pl.ds(at(t, LANES), LANES)] = placed[pl.ds(row * HALF + t, 8, stride=HALF), :]
        return carry

    lax.fori_loop(0, HALF, fold, 0, unroll=2)

    @pl.when(my_slab < slabs - 1)
    def _():
        up.wait_send()

    @pl.when(my_slab > 0)
    def _():
        down.wait_send()


def per_device(slabs, doms, state, send_index, send_count, slot_target, cross_mass, mass, new_order):
    cap = send_index.shape[3]
    new_count = mass.shape[1]
    group = new_count // doms
    slots = doms * cap
    pool_rows = (state.shape[1] + 2 * RIM) * HALF
    rim_rows = RIM * HALF
    code_rows = -(-group * HALF // 16) * 16
    devices = slabs * doms
    steps = ITERS
    vmem, smem = pltpu.VMEM, pltpu.SMEM
    dma = pltpu.SemaphoreType.DMA
    field = vmem((new_count * HALF, LANES), F32)
    scratch = [
        vmem((pool_rows, LANES), F32),
        *[vmem((rim_rows, LANES), BF16)] * 4,
        vmem((slots * HALF, LANES), BF16),
        vmem((slots * HALF, LANES), BF16),
        vmem((8 * LANES, LANES), F32),
        vmem((slots // 2 * LANES, LANES), BF16),
        vmem((new_count // 2 * LANES, 2 * LANES), BF16),
        vmem((slots * HALF, LANES), F32),
        *[field] * 5,
        vmem((doms * code_rows, LANES), jnp.int16),
        vmem((doms * code_rows, LANES), jnp.int16),
        vmem((doms, LANES), F32),
        vmem((doms, LANES), F32),
        field,
        vmem((8, LANES), F32),
        vmem((steps, devices, LANES), F32),
        dma((2,)), dma((2,)), dma((doms,)), dma((doms,)),
        dma((steps, devices)), dma((steps, devices)),
        dma((doms,)), dma((doms,)), dma((doms,)), dma((doms,)),
    ]
    out = pl.pallas_call(
        functools.partial(kernel, slabs, doms, cap, group),
        out_shape=jax.ShapeDtypeStruct((new_count, V * Q), F32),
        in_specs=[pl.BlockSpec(memory_space=smem)] * 3 + [pl.BlockSpec(memory_space=vmem)] * 4,
        out_specs=pl.BlockSpec(memory_space=vmem),
        scratch_shapes=scratch,
        compiler_params=pltpu.CompilerParams(
            collective_id=0, has_side_effects=True, vmem_limit_bytes=48 * 1024 * 1024
        ),
        cost_estimate=pl.CostEstimate(flops=10**9, bytes_accessed=4 * 10**6, transcendentals=0),
    )(
        send_index[0, 0], send_count[0], new_order[0], slot_target[0],
        state[0], cross_mass[0, 0], mass[0],
    )
    return out[None]


def solution(mesh):
    in_specs = (
        P("dom", "slab", None),
        P("dom", "slab", None, None),
        P("dom", "slab", None),
        P("dom", "slab", None),
        P("dom", "slab", None, None),
        P("dom", "slab", None),
        P("dom", "slab", None),
    )
    return jax.shard_map(
        functools.partial(per_device, mesh.shape["slab"], mesh.shape["dom"]),
        mesh=mesh, in_specs=in_specs, out_specs=P("dom", "slab", None), check_vma=False,
    )
```

time: 294 us -> 67.3 us (0.23)
  the two profiles are of different devices: /device:TPU:0 before, /device:TPU:27 now
where the time goes in v1:
time: 67.3 us; the launch traced here: 67 us
  Pallas kernels  61.6 us (92%)
  local copies, waits for them, and re-layouts  5.44 us (8%)
    pallas_call x1, Pallas kernels, per_device(): pl.pallas_call(functools.partial(kernel, slabs, doms, cap, group), out_sh...  61.6 us
    unnamed x15, local copies, waits for them, and re-layouts  5.36 us

profile of v1, /device:TPU:27, one launch (start us, length us, event | category | flops | bytes accessed | tf_op | source)
XLA Modules:
  0.0 67.0 jit_solution(2880102929371979655)
XLA Ops:
  0.0 0.0 copy-start.6
  0.0 0.7 %copy-done.6 = s32[1,1,16,4]{2,3,1,0:T(4,128)S(1)} copy-done((s32[1,1,16,4]{2,3,1,0:T(4,128)S(1)}, s32[1,1,16,4]{2,3,1,0:T(4,128)}, u32[]{:S(2)}) %copy-start.6) | copy-done | bytes 280
  0.7 0.0 copy-start.3
  0.7 0.0 copy-start.4
  0.7 0.0 copy-start.5
  0.7 0.1 copy.8.index_ref
  0.8 0.6 copy-done.3
  1.3 0.0 copy-done.4
  1.4 0.0 copy-done.5
  1.4 0.0 copy-start
  1.4 1.2 %copy-done = f32[1,64,4096]{2,1,0:T(8,128)S(1)} copy-done((f32[1,64,4096]{2,1,0:T(8,128)S(1)}, f32[1,64,4096]{2,1,0:T(8,128)}, u32[]{:S(2)}) %copy-start) | copy-done | bytes 1048600
  2.6 0.0 copy-start.1
  2.6 1.0 %copy-done.1 = bf16[1,1,64,4096]{3,2,1,0:T(8,128)(2,1)S(1)} copy-done((bf16[1,1,64,4096]{3,2,1,0:T(8,128)(2,1)S(1)}, bf16[1,1,64,4096]{3,2,1,0:T(8,128)(2,1)}, u32[]{:S(2)}) %copy-start.1) | copy-done | bytes 524312
  3.6 0.0 copy-start.2
  3.6 0.9 %copy-done.2 = bf16[1,32,3072]{2,1,0:T(8,128)(2,1)S(1)} copy-done((bf16[1,32,3072]{2,1,0:T(8,128)(2,1)S(1)}, bf16[1,32,3072]{2,1,0:T(8,128)(2,1)}, u32[]{:S(2)}) %copy-start.2) | copy-done | bytes 196632
  4.6 61.6 %shard_map.73 = f32[64,3072]{1,0:T(8,128)S(1)} custom-call(s32[16,4]{1,0:T(8,128)S(1)} %copy.8.index_ref, s32[1,16]{1,0:T(1,128)S(1)} %bitcast.12, s32[1,64]{1,0:T(1,128)S(1)} %bitcast.13, s32[1,64]{1,0:T(1,128)S(1)} %bitcast.14, bf16[32,3072]{1,0:T(8,128)(2,1)S(1)} %bitcast.11, bf16[64,4096]{1,0:T(8,128)(2,1)S(1)} %bitcast.10, f32[64,4096]{1,0:T(8,128)S(1)} %bitcast.9), custom_call_target="tpu_custom_call" | custom-call | flops 1000000000 | bytes 4000000 | tf_op jit(solution)/shard_map/pallas_call | solution.py:459
  66.2 0.9 %copy.10 = f32[1,64,3072]{2,1,0:T(8,128)} copy(f32[1,64,3072]{2,1,0:T(8,128)S(1)} %bitcast.8) | data formatting | bytes 1572864
Async XLA Ops:
  0.0 0.7 %copy-start.6 = (s32[1,1,16,4]{2,3,1,0:T(4,128)S(1)}, s32[1,1,16,4]{2,3,1,0:T(4,128)}, u32[]{:S(2)}) copy-start(s32[1,1,16,4]{2,3,1,0:T(4,128)} %param.8) | copy-start | bytes 772
  0.7 0.7 copy-start.3
  0.7 0.7 copy-start.4
  0.7 0.7 %copy-start.5 = (s32[1,1,64]{2,1,0:T(1,128)S(1)}, s32[1,1,64]{2,1,0:T(1,128)}, u32[]{:S(2)}) copy-start(s32[1,1,64]{2,1,0:T(1,128)} %param.10) | copy-start | bytes 772
  1.4 1.2 %copy-start = (f32[1,64,4096]{2,1,0:T(8,128)S(1)}, f32[1,64,4096]{2,1,0:T(8,128)}, u32[]{:S(2)}) copy-start(f32[1,64,4096]{2,1,0:T(8,128)} %param.12) | copy-start | bytes 3145732
  2.6 1.0 %copy-start.1 = (bf16[1,1,64,4096]{3,2,1,0:T(8,128)(2,1)S(1)}, bf16[1,1,64,4096]{3,2,1,0:T(8,128)(2,1)}, u32[]{:S(2)}) copy-start(bf16[1,1,64,4096]{3,2,1,0:T(8,128)(2,1)} %param.11) | copy-start | bytes 1572868
  3.6 0.9 %copy-start.2 = (bf16[1,32,3072]{2,1,0:T(8,128)(2,1)S(1)}, bf16[1,32,3072]{2,1,0:T(8,128)(2,1)}, u32[]{:S(2)}) copy-start(bf16[1,32,3072]{2,1,0:T(8,128)(2,1)} %param.7) | copy-start | bytes 589828

commit v2 on v1

--- a/solution.py
+++ b/solution.py
@@ -72,8 +72,9 @@
 
 def kernel(
     slabs, doms, cap, group,
-    index_ref, count_ref, order_ref, target_ref, state_ref, cross_ref, mass_ref,
+    index_ref, count_ref, order_ref, target_ref, state_hbm, cross_hbm, mass_hbm,
     out_ref,
+    state_ref, cross_ref, mass_ref, load_sem,
     pool, up_out, down_out, up_in, down_in, packets, received, block, cross, blocks,
     contrib, residual, direction, image, answer, element, codes, codes_in, scales, scales_in,
     placed, sums, sums_in,
@@ -93,6 +94,14 @@
         there = lax.rem(me + i, devices)
         return {"slab": lax.div(there, doms), "dom": lax.rem(there, doms)}
 
+    loads = [
+        pltpu.make_async_copy(src, dst, load_sem.at[n])
+        for n, (src, dst) in enumerate(
+            ((state_hbm, state_ref), (mass_hbm, mass_ref), (cross_hbm, cross_ref))
+        )
+    ]
+    for load in loads:
+        load.start()
     barrier = pltpu.get_barrier_semaphore()
 
     def greet(i, carry):
@@ -100,6 +109,8 @@
         return carry
 
     lax.fori_loop(1, devices, greet, 0)
+
+    loads[0].wait()
 
     def unfold(t, carry):
         for row in range(0, elements, 16):
@@ -132,6 +143,8 @@
     def _():
         down.start()
 
+    loads[1].wait()
+
     def prepare_mass(j, carry):
         pair_blocks(mass_ref, j, block)
 
@@ -141,7 +154,7 @@
             blocks[pl.ds(at(j * 8 + i, LANES), LANES), LANES:2 * LANES] = low
             return inner
 
-        return lax.fori_loop(0, 8, cut, carry)
+        return lax.fori_loop(0, 8, cut, carry, unroll=4)
 
     lax.fori_loop(0, new_count // 32, prepare_mass, 0)
 
@@ -167,7 +180,7 @@
         live = count_ref[0, dom]
         rows = []
         for c in range(cap):
-            row = pool[pl.ds(index_ref[dom, c] * HALF, HALF), :]
+            row = pool[pl.ds(index_ref[c, dom] * HALF, HALF), :]
             rows.append(row * jnp.minimum(jnp.maximum(live - c, 0), 1).astype(F32))
         return jnp.concatenate(rows, axis=0).astype(BF16)
 
@@ -179,8 +192,11 @@
             device_id={"slab": my_slab, "dom": dom}, device_id_type=pl.DeviceIdType.MESH,
         )
 
+    def partner(i):
+        return lax.rem(my_dom + 1 + lax.rem(i + doms // 2 - 2, doms - 1), doms)
+
     def send_packet(i, carry):
-        dom = lax.rem(my_dom + i, doms)
+        dom = partner(i)
         packets[pl.ds(at(dom, chunk), chunk), :] = pick(dom)
         packet(dom).start()
         return carry
@@ -194,11 +210,14 @@
         pair_blocks(cross_ref, j, block)
 
         def cut(i, inner):
-            cross[pl.ds(at(j * 8 + i, LANES), LANES), :] = block[pl.ds(at(i, LANES), LANES), :].astype(BF16)
+            cross[pl.ds(at(j * 8 + i, LANES), LANES), :] = jnp.transpose(
+                block[pl.ds(at(i, LANES), LANES), :]
+            ).astype(BF16)
             return inner
 
-        return lax.fori_loop(0, 8, cut, carry)
-
+        return lax.fori_loop(0, 8, cut, carry, unroll=4)
+
+    loads[2].wait()
     lax.fori_loop(0, slots // 16, prepare_cross, 0)
 
     def arrive(dom, carry):
@@ -226,12 +245,12 @@
             pair = j * 8 + h * cap + c
             field = jnp.concatenate(interleave(first[part], second[part]), axis=0).astype(BF16)
             matrix = cross[pl.ds(at(pair, LANES), LANES), :]
-            contrib[pl.ds(at(pair, V), V), :] = lax.dot_general(
-                field, matrix, (((1,), (1,)), ((), ())), preferred_element_type=F32
+            contrib[pl.ds(at(pair, V), V), :] = jnp.dot(
+                field, matrix, preferred_element_type=F32
             )
         return carry
 
-    lax.fori_loop(0, doms // 2, product, 0)
+    lax.fori_loop(0, doms // 2, product, 0, unroll=2)
 
     shape = (new_count, slots)
     onehot = jnp.where(lax.broadcasted_iota(jnp.int32, shape, 0) == target_ref[...], 1.0, 0.0).astype(BF16)
@@ -253,7 +272,7 @@
             residual[pl.ds(j * 8 * V + HALF + t, 8, stride=V), :] = odd
         return carry
 
-    lax.fori_loop(0, HALF, scatter, 0, unroll=2)
+    lax.fori_loop(0, HALF, scatter, 0, unroll=6)
 
     pairs = new_count // 2
 
@@ -270,22 +289,14 @@
             pltpu.make_async_remote_copy(
                 src_ref=sums.at[step:step + 1, :],
                 dst_ref=sums_in.at[step, pl.ds(i - 1, 1), :],
-                send_sem=sum_send.at[step, i - 1], recv_sem=sum_recv.at[step, i - 1],
+                send_sem=sum_send.at[step], recv_sem=sum_recv.at[step],
                 device_id=device(i), device_id_type=pl.DeviceIdType.MESH,
             ).start()
             return carry
 
-        def wait(i, carry):
-            pltpu.make_async_remote_copy(
-                src_ref=sums.at[step:step + 1, :],
-                dst_ref=sums_in.at[step, pl.ds(i - 1, 1), :],
-                send_sem=sum_send.at[step, i - 1], recv_sem=sum_recv.at[step, i - 1],
-                device_id=device(i), device_id_type=pl.DeviceIdType.MESH,
-            ).wait()
-            return carry
-
         lax.fori_loop(1, devices, send, 0)
-        lax.fori_loop(1, devices, wait, 0)
+        arrived = sums_in.at[step, 0:devices - 1, :]
+        pltpu.make_async_copy(arrived, arrived, sum_recv.at[step]).wait()
         total = own + jnp.sum(sums_in[step, 0:devices - 1, :], axis=0, keepdims=True)
         column = row_to_column(total, 2 * V)
         return column[:V], column[V:]
@@ -300,7 +311,7 @@
         image[at_pair, :] = w
         return rr + r * r, rw + r * w
 
-    rr, rw = all_sum(0, *lax.fori_loop(0, pairs, first_pass, (zero, zero), unroll=2))
+    rr, rw = all_sum(0, *lax.fori_loop(0, pairs, first_pass, (zero, zero), unroll=8))
     alpha = rr / rw
 
     def second_pass(pair, carry):
@@ -316,7 +327,7 @@
         return nn + r * r, nw + r * w
 
     contrib_w = element
-    nn, nw = all_sum(1, *lax.fori_loop(0, pairs, second_pass, (zero, zero), unroll=2))
+    nn, nw = all_sum(1, *lax.fori_loop(0, pairs, second_pass, (zero, zero), unroll=8))
     beta = nn / rr
     alpha = nn / (nw - beta * nn / alpha)
     rr = nn
@@ -334,7 +345,7 @@
         w = apply_mass(pair, r)
         return nn + r * r, nw + r * w
 
-    nn, nw = all_sum(2, *lax.fori_loop(0, pairs, third_pass, (zero, zero), unroll=2))
+    nn, nw = all_sum(2, *lax.fori_loop(0, pairs, third_pass, (zero, zero), unroll=8))
     beta = nn / rr
     alpha = nn / (nw - beta * nn / alpha)
 
@@ -348,7 +359,7 @@
         element[pl.ds(at(number + 8, HALF), HALF), :] = second
         return carry
 
-    lax.fori_loop(0, pairs, last_pass, 0, unroll=2)
+    lax.fori_loop(0, pairs, last_pass, 0, unroll=4)
 
     used = group * HALF
 
@@ -380,7 +391,7 @@
         ]
 
     def send_code(i, carry):
-        dom = lax.rem(my_dom + i, doms)
+        dom = partner(i)
         coded, scale = code(dom)
         codes[pl.ds(at(dom, code_rows), code_rows), :] = coded
         scales[pl.ds(dom, 1), :] = scale
@@ -412,6 +423,10 @@
         return carry
 
     lax.fori_loop(0, HALF, fold, 0, unroll=2)
+
+    for step in range(ITERS):
+        left = sums_in.at[step, 0:devices - 1, :]
+        pltpu.make_async_copy(left, left, sum_send.at[step]).wait()
 
     @pl.when(my_slab < slabs - 1)
     def _():
@@ -436,6 +451,10 @@
     dma = pltpu.SemaphoreType.DMA
     field = vmem((new_count * HALF, LANES), F32)
     scratch = [
+        vmem(state.shape[1:], BF16),
+        vmem((slots, Q * Q), BF16),
+        vmem((new_count, Q * Q), F32),
+        dma((3,)),
         vmem((pool_rows, LANES), F32),
         *[vmem((rim_rows, LANES), BF16)] * 4,
         vmem((slots * HALF, LANES), BF16),
@@ -453,13 +472,14 @@
         vmem((8, LANES), F32),
         vmem((steps, devices, LANES), F32),
         dma((2,)), dma((2,)), dma((doms,)), dma((doms,)),
-        dma((steps, devices)), dma((steps, devices)),
+        dma((steps,)), dma((steps,)),
         dma((doms,)), dma((doms,)), dma((doms,)), dma((doms,)),
     ]
     out = pl.pallas_call(
         functools.partial(kernel, slabs, doms, cap, group),
         out_shape=jax.ShapeDtypeStruct((new_count, V * Q), F32),
-        in_specs=[pl.BlockSpec(memory_space=smem)] * 3 + [pl.BlockSpec(memory_space=vmem)] * 4,
+        in_specs=[pl.BlockSpec(memory_space=smem)] * 3 + [pl.BlockSpec(memory_space=vmem)]
+        + [pl.BlockSpec(memory_space=pltpu.HBM)] * 3,
         out_specs=pl.BlockSpec(memory_space=vmem),
         scratch_shapes=scratch,
         compiler_params=pltpu.CompilerParams(
@@ -467,7 +487,7 @@
         ),
         cost_estimate=pl.CostEstimate(flops=10**9, bytes_accessed=4 * 10**6, transcendentals=0),
     )(
-        send_index[0, 0], send_count[0], new_order[0], slot_target[0],
+        send_index[0, 0].T, send_count[0], new_order[0], slot_target[0],
         state[0], cross_mass[0, 0], mass[0],
     )
     return out[None]

time: 67.3 us -> 58 us (0.86)
  the two profiles are of different devices: /device:TPU:27 before, /device:TPU:0 now
where the time goes in v2:
time: 58 us; the launch traced here: 57.8 us
  Pallas kernels  53 us (91%)
  local copies, waits for them, and re-layouts  4.77 us (8%)
    pallas_call x1, Pallas kernels, per_device(): pl.pallas_call(functools.partial(kernel, slabs, doms, cap, group), out_sh...  53 us
    unnamed x15, local copies, waits for them, and re-layouts  4.77 us

profile of v2, /device:TPU:0, one launch (start us, length us, event | category | flops | bytes accessed | tf_op | source)
XLA Modules:
  0.0 57.8 jit_solution(5119320309314770767)
XLA Ops:
  0.0 0.0 copy-start.3
  0.0 0.0 copy-start.4
  0.0 0.0 copy-start.5
  0.0 0.0 copy-start.6
  0.0 0.7 %copy-done.3 = s32[1,1,16,4]{2,3,1,0:T(4,128)S(1)} copy-done((s32[1,1,16,4]{2,3,1,0:T(4,128)S(1)}, s32[1,1,16,4]{2,3,1,0:T(4,128)}, u32[]{:S(2)}) %copy-start.3) | copy-done | bytes 280
  0.7 0.0 copy-done.4
  0.7 0.0 copy-done.5
  0.7 0.0 copy-done.6
  0.7 0.0 copy-start
  0.7 1.2 %copy-done = f32[1,64,4096]{2,1,0:T(8,128)S(1)} copy-done((f32[1,64,4096]{2,1,0:T(8,128)S(1)}, f32[1,64,4096]{2,1,0:T(8,128)}, u32[]{:S(2)}) %copy-start) | copy-done | bytes 1048600
  1.9 0.0 copy-start.1
  1.9 1.0 %copy-done.1 = bf16[1,1,64,4096]{3,2,1,0:T(8,128)(2,1)S(1)} copy-done((bf16[1,1,64,4096]{3,2,1,0:T(8,128)(2,1)S(1)}, bf16[1,1,64,4096]{3,2,1,0:T(8,128)(2,1)}, u32[]{:S(2)}) %copy-start.1) | copy-done | bytes 524312
  3.0 0.0 copy-start.2
  3.0 0.9 %copy-done.2 = bf16[1,32,3072]{2,1,0:T(8,128)(2,1)S(1)} copy-done((bf16[1,32,3072]{2,1,0:T(8,128)(2,1)S(1)}, bf16[1,32,3072]{2,1,0:T(8,128)(2,1)}, u32[]{:S(2)}) %copy-start.2) | copy-done | bytes 196632
  3.9 53.0 %shard_map.73 = f32[64,3072]{1,0:T(8,128)S(1)} custom-call(s32[4,16]{1,0:T(4,128)S(1)} %bitcast.14, s32[1,16]{1,0:T(1,128)S(1)} %bitcast.15, s32[1,64]{1,0:T(1,128)S(1)} %bitcast.16, s32[1,64]{1,0:T(1,128)S(1)} %bitcast.17, bf16[32,3072]{1,0:T(8,128)(2,1)S(1)} %bitcast.13, bf16[64,4096]{1,0:T(8,128)(2,1)S(1)} %bitcast.12, f32[64,4096]{1,0:T(8,128)S(1)} %bitcast.11), custom_call_target="tpu_custom_call" | custom-call | flops 1000000000 | bytes 4000000 | tf_op jit(solution)/shard_map/pallas_call | solution.py:478
  56.9 0.9 %copy.9 = f32[1,64,3072]{2,1,0:T(8,128)} copy(f32[1,64,3072]{2,1,0:T(8,128)S(1)} %bitcast.10) | data formatting | bytes 1572864
Async XLA Ops:
  0.0 0.7 %copy-start.3 = (s32[1,1,16,4]{2,3,1,0:T(4,128)S(1)}, s32[1,1,16,4]{2,3,1,0:T(4,128)}, u32[]{:S(2)}) copy-start(s32[1,1,16,4]{2,3,1,0:T(4,128)} %param.8) | copy-start | bytes 772
  0.0 0.7 %copy-start.4 = (s32[1,1,16]{2,1,0:T(1,128)S(1)}, s32[1,1,16]{2,1,0:T(1,128)}, u32[]{:S(2)}) copy-start(s32[1,1,16]{2,1,0:T(1,128)} %param.9) | copy-start | bytes 196
  0.0 0.7 %copy-start.5 = (s32[1,1,64]{2,1,0:T(1,128)S(1)}, s32[1,1,64]{2,1,0:T(1,128)}, u32[]{:S(2)}) copy-start(s32[1,1,64]{2,1,0:T(1,128)} %param.13) | copy-start | bytes 772
  0.0 0.7 %copy-start.6 = (s32[1,1,64]{2,1,0:T(1,128)S(1)}, s32[1,1,64]{2,1,0:T(1,128)}, u32[]{:S(2)}) copy-start(s32[1,1,64]{2,1,0:T(1,128)} %param.10) | copy-start | bytes 772
  0.7 1.2 %copy-start = (f32[1,64,4096]{2,1,0:T(8,128)S(1)}, f32[1,64,4096]{2,1,0:T(8,128)}, u32[]{:S(2)}) copy-start(f32[1,64,4096]{2,1,0:T(8,128)} %param.12) | copy-start | bytes 3145732
  1.9 1.0 %copy-start.1 = (bf16[1,1,64,4096]{3,2,1,0:T(8,128)(2,1)S(1)}, bf16[1,1,64,4096]{3,2,1,0:T(8,128)(2,1)}, u32[]{:S(2)}) copy-start(bf16[1,1,64,4096]{3,2,1,0:T(8,128)(2,1)} %param.11) | copy-start | bytes 1572868
  3.0 0.9 %copy-start.2 = (bf16[1,32,3072]{2,1,0:T(8,128)(2,1)S(1)}, bf16[1,32,3072]{2,1,0:T(8,128)(2,1)}, u32[]{:S(2)}) copy-start(bf16[1,32,3072]{2,1,0:T(8,128)(2,1)} %param.7) | copy-start | bytes 589828

commit v3 on v2

--- a/solution.py
+++ b/solution.py
@@ -76,7 +76,7 @@
     out_ref,
     state_ref, cross_ref, mass_ref, load_sem,
     pool, up_out, down_out, up_in, down_in, packets, received, block, cross, blocks,
-    contrib, residual, direction, image, answer, element, codes, codes_in, scales, scales_in,
+    contrib, residual, image, z_ref, next_residual, next_image, flat_x, flat_p, flat_r, codes, codes_in, scales, scales_in,
     placed, sums, sums_in,
     halo_send, halo_recv, packet_send, packet_recv, sum_send, sum_recv,
     code_send, code_recv, scale_send, scale_recv,
@@ -250,7 +250,7 @@
             )
         return carry
 
-    lax.fori_loop(0, doms // 2, product, 0, unroll=2)
+    lax.fori_loop(0, doms // 2, product, 0, unroll=4)
 
     shape = (new_count, slots)
     onehot = jnp.where(lax.broadcasted_iota(jnp.int32, shape, 0) == target_ref[...], 1.0, 0.0).astype(BF16)
@@ -281,7 +281,7 @@
         result = jnp.dot(terms, blocks[pl.ds(at(pair, LANES), LANES), :], preferred_element_type=F32)
         return (result[V:, :LANES] + result[:V, LANES:]) + result[:V, :LANES]
 
-    def all_sum(step, left, right):
+    def sum_start(step, left, right):
         own = column_to_row(jnp.sum(jnp.concatenate([left, right], axis=0), axis=1, keepdims=True))
         sums[step:step + 1, :] = own
 
@@ -295,6 +295,9 @@
             return carry
 
         lax.fori_loop(1, devices, send, 0)
+        return own
+
+    def sum_end(step, own):
         arrived = sums_in.at[step, 0:devices - 1, :]
         pltpu.make_async_copy(arrived, arrived, sum_recv.at[step]).wait()
         total = own + jnp.sum(sums_in[step, 0:devices - 1, :], axis=0, keepdims=True)
@@ -311,23 +314,37 @@
         image[at_pair, :] = w
         return rr + r * r, rw + r * w
 
-    rr, rw = all_sum(0, *lax.fori_loop(0, pairs, first_pass, (zero, zero), unroll=8))
+    own = sum_start(0, *lax.fori_loop(0, pairs, first_pass, (zero, zero), unroll=8))
+
+    def image_of_image(pair, carry):
+        at_pair = pl.ds(at(pair, V), V)
+        z_ref[at_pair, :] = apply_mass(pair, image[at_pair, :])
+        return carry
+
+    lax.fori_loop(0, pairs, image_of_image, 0, unroll=8)
+    rr, rw = sum_end(0, own)
     alpha = rr / rw
 
     def second_pass(pair, carry):
         nn, nw = carry
         at_pair = pl.ds(at(pair, V), V)
-        p = residual[at_pair, :]
-        r = p - alpha * image[at_pair, :]
-        direction[at_pair, :] = p
-        answer[at_pair, :] = alpha * p
-        residual[at_pair, :] = r
-        w = apply_mass(pair, r)
-        contrib_w[at_pair, :] = w
+        s = image[at_pair, :]
+        r = residual[at_pair, :] - alpha * s
+        w = s - alpha * z_ref[at_pair, :]
+        next_residual[at_pair, :] = r
+        next_image[at_pair, :] = w
         return nn + r * r, nw + r * w
 
-    contrib_w = element
-    nn, nw = all_sum(1, *lax.fori_loop(0, pairs, second_pass, (zero, zero), unroll=8))
+    own = sum_start(1, *lax.fori_loop(0, pairs, second_pass, (zero, zero), unroll=4))
+
+    def next_image_of_image(pair, carry):
+        at_pair = pl.ds(at(pair, V), V)
+        contrib[at_pair, :] = apply_mass(pair, next_image[at_pair, :])
+        return carry
+
+    lax.fori_loop(0, pairs, next_image_of_image, 0, unroll=8)
+    nn, nw = sum_end(1, own)
+    first_alpha = alpha
     beta = nn / rr
     alpha = nn / (nw - beta * nn / alpha)
     rr = nn
@@ -335,38 +352,50 @@
     def third_pass(pair, carry):
         nn, nw = carry
         at_pair = pl.ds(at(pair, V), V)
-        r = residual[at_pair, :]
-        p = r + beta * direction[at_pair, :]
-        s = contrib_w[at_pair, :] + beta * image[at_pair, :]
-        direction[at_pair, :] = p
-        answer[at_pair, :] = answer[at_pair, :] + alpha * p
+        b = residual[at_pair, :]
+        r = next_residual[at_pair, :]
+        w = next_image[at_pair, :]
+        p = r + beta * b
+        s = w + beta * image[at_pair, :]
+        z = contrib[at_pair, :] + beta * z_ref[at_pair, :]
+        residual[at_pair, :] = first_alpha * b + alpha * p
+        image[at_pair, :] = p
         r = r - alpha * s
-        residual[at_pair, :] = r
-        w = apply_mass(pair, r)
+        w = w - alpha * z
+        next_residual[at_pair, :] = r
         return nn + r * r, nw + r * w
 
-    nn, nw = all_sum(2, *lax.fori_loop(0, pairs, third_pass, (zero, zero), unroll=8))
+    own = sum_start(2, *lax.fori_loop(0, pairs, third_pass, (zero, zero), unroll=4))
+
+    def flatten(pair, carry):
+        at_pair = pl.ds(at(pair, V), V)
+        number = lax.div(pair, 8) * 16 + lax.rem(pair, 8)
+        for src, dst in ((residual, flat_x), (image, flat_p), (next_residual, flat_r)):
+            value = src[at_pair, :]
+            first, second = interleave(value[:HALF], value[HALF:])
+            dst[pl.ds(at(number, HALF), HALF), :] = first
+            dst[pl.ds(at(number + 8, HALF), HALF), :] = second
+        return carry
+
+    lax.fori_loop(0, pairs, flatten, 0, unroll=4)
+    nn, nw = sum_end(2, own)
     beta = nn / rr
     alpha = nn / (nw - beta * nn / alpha)
 
-    def last_pass(pair, carry):
-        at_pair = pl.ds(at(pair, V), V)
-        p = residual[at_pair, :] + beta * direction[at_pair, :]
-        x = answer[at_pair, :] + alpha * p
-        first, second = interleave(x[:HALF], x[HALF:])
-        number = lax.div(pair, 8) * 16 + lax.rem(pair, 8)
-        element[pl.ds(at(number, HALF), HALF), :] = first
-        element[pl.ds(at(number + 8, HALF), HALF), :] = second
-        return carry
-
-    lax.fori_loop(0, pairs, last_pass, 0, unroll=4)
+    def flat_factor(column):
+        wide = jnp.broadcast_to(column, (V, LANES))
+        return jnp.where(left_half((HALF, LANES)), wide[:HALF], wide[HALF:])
+
+    factor_r = flat_factor(alpha)
+    factor_p = flat_factor(alpha * beta)
 
     used = group * HALF
 
     def code(dom):
-        rows = [
-            element[pl.ds(order_ref[0, dom * group + g] * HALF, HALF), :] for g in range(group)
-        ]
+        rows = []
+        for g in range(group):
+            which = pl.ds(order_ref[0, dom * group + g] * HALF, HALF)
+            rows.append(flat_x[which, :] + (factor_p * flat_p[which, :] + factor_r * flat_r[which, :]))
         value = jnp.concatenate(rows, axis=0)
         top = jnp.maximum(jnp.max(jnp.abs(value), axis=1, keepdims=True), 1e-30)
         coded = jnp.round(value * (LIMIT / top)).astype(jnp.int32)
@@ -404,25 +433,23 @@
     codes_in[pl.ds(at(my_dom, code_rows), code_rows), :] = coded
     scales_in[pl.ds(my_dom, 1), :] = scale
 
-    def place(dom, carry):
-        @pl.when(dom != my_dom)
-        def _():
-            for copy in code_copies(dom, dom, dom):
-                copy.wait()
-
-        value = codes_in[pl.ds(at(dom, code_rows), code_rows), :].astype(jnp.int32).astype(F32)[:used]
-        scale = row_to_column(scales_in[pl.ds(dom, 1), :], used)
-        placed[pl.ds(at(dom, used), used), :] = value * scale
-        return carry
-
-    lax.fori_loop(0, doms, place, 0)
-
-    def fold(t, carry):
-        for row in range(0, new_count, 8):
-            out_ref[row:row + 8, pl.ds(at(t, LANES), LANES)] = placed[pl.ds(row * HALF + t, 8, stride=HALF), :]
-        return carry
-
-    lax.fori_loop(0, HALF, fold, 0, unroll=2)
+    def place(rows, carry):
+        for n in range(8 // group):
+            dom = rows * (8 // group) + n
+
+            @pl.when(dom != my_dom)
+            def _():
+                for copy in code_copies(dom, dom, dom):
+                    copy.wait()
+
+            value = codes_in[pl.ds(at(dom, code_rows), code_rows), :].astype(jnp.int32).astype(F32)[:used]
+            scale = row_to_column(scales_in[pl.ds(dom, 1), :], used)
+            placed[n * used:(n + 1) * used, :] = value * scale
+        for t in range(HALF):
+            out_ref[pl.ds(at(rows, 8), 8), t * LANES:(t + 1) * LANES] = placed[pl.ds(t, 8, stride=HALF), :]
+        return carry
+
+    lax.fori_loop(0, new_count // 8, place, 0)
 
     for step in range(ITERS):
         left = sums_in.at[step, 0:devices - 1, :]
@@ -462,13 +489,13 @@
         vmem((8 * LANES, LANES), F32),
         vmem((slots // 2 * LANES, LANES), BF16),
         vmem((new_count // 2 * LANES, 2 * LANES), BF16),
-        vmem((slots * HALF, LANES), F32),
-        *[field] * 5,
+        vmem((max(slots, new_count) * HALF, LANES), F32),
+        *[field] * 8,
         vmem((doms * code_rows, LANES), jnp.int16),
         vmem((doms * code_rows, LANES), jnp.int16),
         vmem((doms, LANES), F32),
         vmem((doms, LANES), F32),
-        field,
+        vmem((8 * HALF, LANES), F32),
         vmem((8, LANES), F32),
         vmem((steps, devices, LANES), F32),
         dma((2,)), dma((2,)), dma((doms,)), dma((doms,)),
@@ -483,7 +510,7 @@
         out_specs=pl.BlockSpec(memory_space=vmem),
         scratch_shapes=scratch,
         compiler_params=pltpu.CompilerParams(
-            collective_id=0, has_side_effects=True, vmem_limit_bytes=48 * 1024 * 1024
+            collective_id=0, has_side_effects=True, vmem_limit_bytes=56 * 1024 * 1024
         ),
         cost_estimate=pl.CostEstimate(flops=10**9, bytes_accessed=4 * 10**6, transcendentals=0),
     )(

time: 58 us -> 53.2 us (0.917)
  local copies, waits for them, and re-layouts: 4.77 us -> 2.07 us
  Pallas kernels: 53 us -> 51 us
    unnamed x15 -> x1, local copies, waits for them, and re-layouts: 4.77 us -> 2.07 us
    pallas_call x1, Pallas kernels: 53 us -> 51 us  [per_device(): pl.pallas_call(functools.partial(kernel, slabs, doms, cap, group), out_sh...]
where the time goes in v3:
time: 53.2 us; the launch traced here: 53.1 us
  Pallas kernels  51 us (96%)
  local copies, waits for them, and re-layouts  2.07 us (4%)
    pallas_call x1, Pallas kernels, per_device(): pl.pallas_call(functools.partial(kernel, slabs, doms, cap, group), out_sh...  51 us
    unnamed x1, local copies, waits for them, and re-layouts  2.07 us

profile of v3, /device:TPU:0, one launch (start us, length us, event | category | flops | bytes accessed | tf_op | source)
XLA Modules:
  0.0 53.1 jit_solution(6418022419188063582)
XLA Ops:
  0.0 51.0 %shard_map.73 = f32[64,3072]{1,0:T(8,128)} custom-call(s32[4,16]{1,0:T(4,128)} %bitcast.14, s32[1,16]{1,0:T(1,128)} %bitcast.15, s32[1,64]{1,0:T(1,128)} %bitcast.16, s32[1,64]{1,0:T(1,128)} %bitcast.17, bf16[32,3072]{1,0:T(8,128)(2,1)} %bitcast.13, bf16[64,4096]{1,0:T(8,128)(2,1)} %bitcast.12, f32[64,4096]{1,0:T(8,128)} %bitcast.11), custom_call_target="tpu_custom_call" | custom-call | flops 1000000000 | bytes 4000000 | tf_op jit(solution)/shard_map/pallas_call | solution.py:505
  51.0 2.1 %copy.9 = f32[1,64,3072]{2,1,0:T(8,128)} copy(f32[1,64,3072]{2,1,0:T(8,128)} %bitcast.10) | data formatting | bytes 1572864

commit v4 on v3

--- a/solution.py
+++ b/solution.py
@@ -12,7 +12,8 @@
 RIM = 8
 LANES = 128
 HALF = V // 2
-ITERS = 3
+SUMS = 2
+FLOOR = 1e-4
 F32 = jnp.float32
 BF16 = jnp.bfloat16
 LIMIT = 32767.0
@@ -76,7 +77,7 @@
     out_ref,
     state_ref, cross_ref, mass_ref, load_sem,
     pool, up_out, down_out, up_in, down_in, packets, received, block, cross, blocks,
-    contrib, residual, image, z_ref, next_residual, next_image, flat_x, flat_p, flat_r, codes, codes_in, scales, scales_in,
+    contrib, residual, image, image2, image3, flat_x, flat_p, flat_r, codes, codes_in, scales, scales_in,
     placed, sums, sums_in,
     halo_send, halo_recv, packet_send, packet_recv, sum_send, sum_recv,
     code_send, code_recv, scale_send, scale_recv,
@@ -281,14 +282,15 @@
         result = jnp.dot(terms, blocks[pl.ds(at(pair, LANES), LANES), :], preferred_element_type=F32)
         return (result[V:, :LANES] + result[:V, LANES:]) + result[:V, :LANES]
 
-    def sum_start(step, left, right):
-        own = column_to_row(jnp.sum(jnp.concatenate([left, right], axis=0), axis=1, keepdims=True))
-        sums[step:step + 1, :] = own
+    def sum_start(step, parts):
+        stack = jnp.sum(jnp.concatenate(parts, axis=0), axis=1, keepdims=True)
+        half = stack.shape[0] // 2
+        own = jnp.concatenate([column_to_row(stack[:half]), column_to_row(stack[half:])], axis=0)
+        sums[step] = own
 
         def send(i, carry):
             pltpu.make_async_remote_copy(
-                src_ref=sums.at[step:step + 1, :],
-                dst_ref=sums_in.at[step, pl.ds(i - 1, 1), :],
+                src_ref=sums.at[step], dst_ref=sums_in.at[step, i - 1],
                 send_sem=sum_send.at[step], recv_sem=sum_recv.at[step],
                 device_id=device(i), device_id_type=pl.DeviceIdType.MESH,
             ).start()
@@ -297,80 +299,74 @@
         lax.fori_loop(1, devices, send, 0)
         return own
 
-    def sum_end(step, own):
-        arrived = sums_in.at[step, 0:devices - 1, :]
+    def sum_end(step, own, count):
+        arrived = sums_in.at[step, 0:devices - 1]
         pltpu.make_async_copy(arrived, arrived, sum_recv.at[step]).wait()
-        total = own + jnp.sum(sums_in[step, 0:devices - 1, :], axis=0, keepdims=True)
-        column = row_to_column(total, 2 * V)
-        return column[:V], column[V:]
+        total = own + jnp.sum(sums_in[step, 0:devices - 1], axis=0)
+        half = count * V // 2
+        column = jnp.concatenate([row_to_column(total[:1], half), row_to_column(total[1:], half)], axis=0)
+        return [column[n * V:(n + 1) * V] for n in range(count)]
 
     zero = jnp.zeros((V, LANES), F32)
+    small = jnp.zeros((HALF, LANES), F32)
 
     def first_pass(pair, carry):
-        rr, rw = carry
-        at_pair = pl.ds(at(pair, V), V)
-        r = residual[at_pair, :]
-        w = apply_mass(pair, r)
-        image[at_pair, :] = w
-        return rr + r * r, rw + r * w
-
-    own = sum_start(0, *lax.fori_loop(0, pairs, first_pass, (zero, zero), unroll=8))
-
-    def image_of_image(pair, carry):
-        at_pair = pl.ds(at(pair, V), V)
-        z_ref[at_pair, :] = apply_mass(pair, image[at_pair, :])
-        return carry
-
-    lax.fori_loop(0, pairs, image_of_image, 0, unroll=8)
-    rr, rw = sum_end(0, own)
-    alpha = rr / rw
-
-    def second_pass(pair, carry):
-        nn, nw = carry
-        at_pair = pl.ds(at(pair, V), V)
-        s = image[at_pair, :]
-        r = residual[at_pair, :] - alpha * s
-        w = s - alpha * z_ref[at_pair, :]
-        next_residual[at_pair, :] = r
-        next_image[at_pair, :] = w
-        return nn + r * r, nw + r * w
-
-    own = sum_start(1, *lax.fori_loop(0, pairs, second_pass, (zero, zero), unroll=4))
-
-    def next_image_of_image(pair, carry):
-        at_pair = pl.ds(at(pair, V), V)
-        contrib[at_pair, :] = apply_mass(pair, next_image[at_pair, :])
-        return carry
-
-    lax.fori_loop(0, pairs, next_image_of_image, 0, unroll=8)
-    nn, nw = sum_end(1, own)
-    first_alpha = alpha
-    beta = nn / rr
-    alpha = nn / (nw - beta * nn / alpha)
-    rr = nn
-
-    def third_pass(pair, carry):
-        nn, nw = carry
+        bb, bw, ww, wq = carry
         at_pair = pl.ds(at(pair, V), V)
         b = residual[at_pair, :]
-        r = next_residual[at_pair, :]
-        w = next_image[at_pair, :]
-        p = r + beta * b
-        s = w + beta * image[at_pair, :]
-        z = contrib[at_pair, :] + beta * z_ref[at_pair, :]
-        residual[at_pair, :] = first_alpha * b + alpha * p
-        image[at_pair, :] = p
-        r = r - alpha * s
-        w = w - alpha * z
-        next_residual[at_pair, :] = r
-        return nn + r * r, nw + r * w
-
-    own = sum_start(2, *lax.fori_loop(0, pairs, third_pass, (zero, zero), unroll=4))
+        w = apply_mass(pair, b)
+        image[at_pair, :] = w
+        q = apply_mass(pair, w)
+        image2[at_pair, :] = q
+        return bb + b * b, bw + b * w, ww + w * w, wq + w * q
+
+    own = sum_start(0, lax.fori_loop(0, pairs, first_pass, (zero,) * 4, unroll=8))
+
+    def third_image(pair, carry):
+        at_pair = pl.ds(at(pair, V), V)
+        image3[at_pair, :] = apply_mass(pair, image2[at_pair, :])
+        return carry
+
+    lax.fori_loop(0, pairs, third_image, 0, unroll=8)
+    bb, bw, ww, wq = sum_end(0, own, 4)
+
+    alpha = bb / bw
+    norm = alpha * (alpha * ww) - bb
+    weighted = bw - 2.0 * (alpha * ww) + alpha * (alpha * wq)
+    beta = norm / bb
+    curve = weighted - beta * (norm / alpha)
+    sound = jnp.logical_and(norm > FLOOR * bb, curve > 0.0)
+    beta = jnp.where(sound, beta, 0.0)
+    alpha1 = jnp.where(sound, norm / jnp.where(sound, curve, 1.0), alpha)
+
+    dots = []
+    for part in range(2):
+        rows = slice(part * HALF, (part + 1) * HALF)
+        a0, a1, grow = (
+            jnp.broadcast_to(value[rows], (HALF, LANES)) for value in (alpha, alpha1, 1.0 + beta)
+        )
+
+        def second_pass(pair, carry, part=part, a0=a0, a1=a1, grow=grow):
+            rr, rw, rs, ps, rp = carry
+            at_pair = pl.ds(at(pair * 2 + part, HALF), HALF)
+            b, w, q, t = (ref[at_pair, :] for ref in (residual, image, image2, image3))
+            p = grow * b - a0 * w
+            s = grow * w - a0 * q
+            r = (b - a0 * w) - a1 * s
+            v = (w - a0 * q) - a1 * (grow * q - a0 * t)
+            image3[at_pair, :] = a0 * b + a1 * p
+            image2[at_pair, :] = p
+            residual[at_pair, :] = r
+            return rr + r * r, rw + r * v, rs + r * s, ps + p * s, rp + r * p
+
+        dots.append(lax.fori_loop(0, pairs, second_pass, (small,) * 5, unroll=4))
+
+    own = sum_start(1, [half for pair in zip(*dots) for half in pair])
 
     def flatten(pair, carry):
         at_pair = pl.ds(at(pair, V), V)
         number = lax.div(pair, 8) * 16 + lax.rem(pair, 8)
-        for src, dst in ((residual, flat_x), (image, flat_p), (next_residual, flat_r)):
+        for src, dst in ((image3, flat_x), (image2, flat_p), (residual, flat_r)):
             value = src[at_pair, :]
             first, second = interleave(value[:HALF], value[HALF:])
             dst[pl.ds(at(number, HALF), HALF), :] = first
@@ -378,9 +374,9 @@
         return carry
 
     lax.fori_loop(0, pairs, flatten, 0, unroll=4)
-    nn, nw = sum_end(2, own)
-    beta = nn / rr
-    alpha = nn / (nw - beta * nn / alpha)
+    rr, rw, rs, ps, rp = sum_end(1, own, 5)
+    beta = -rs / ps
+    alpha = (rr + beta * rp) / (rw + beta * (2.0 * rs + beta * ps))
 
     def flat_factor(column):
         wide = jnp.broadcast_to(column, (V, LANES))
@@ -451,8 +447,8 @@
 
     lax.fori_loop(0, new_count // 8, place, 0)
 
-    for step in range(ITERS):
-        left = sums_in.at[step, 0:devices - 1, :]
+    for step in range(SUMS):
+        left = sums_in.at[step, 0:devices - 1]
         pltpu.make_async_copy(left, left, sum_send.at[step]).wait()
 
     @pl.when(my_slab < slabs - 1)
@@ -462,6 +458,31 @@
     @pl.when(my_slab > 0)
     def _():
         down.wait_send()
+
+
+def move_kernel(src, dst, sem):
+    rows = src.shape[0] // 8
+    copies = [
+        pltpu.make_async_copy(
+            src.at[n * rows:(n + 1) * rows, :], dst.at[n * rows:(n + 1) * rows, :], sem.at[n]
+        )
+        for n in range(8)
+    ]
+    for copy in copies:
+        copy.start()
+    for copy in copies:
+        copy.wait()
+
+
+def move(value):
+    return pl.pallas_call(
+        move_kernel,
+        out_shape=jax.ShapeDtypeStruct(value.shape, value.dtype),
+        in_specs=[pl.BlockSpec(memory_space=pl.ANY)],
+        out_specs=pl.BlockSpec(memory_space=pl.ANY),
+        scratch_shapes=[pltpu.SemaphoreType.DMA((8,))],
+        compiler_params=pltpu.CompilerParams(vmem_limit_bytes=56 * 1024 * 1024),
+    )(value)
 
 
 def per_device(slabs, doms, state, send_index, send_count, slot_target, cross_mass, mass, new_order):
@@ -473,7 +494,7 @@
     rim_rows = RIM * HALF
     code_rows = -(-group * HALF // 16) * 16
     devices = slabs * doms
-    steps = ITERS
+    steps = SUMS
     vmem, smem = pltpu.VMEM, pltpu.SMEM
     dma = pltpu.SemaphoreType.DMA
     field = vmem((new_count * HALF, LANES), F32)
@@ -489,15 +510,15 @@
         vmem((8 * LANES, LANES), F32),
         vmem((slots // 2 * LANES, LANES), BF16),
         vmem((new_count // 2 * LANES, 2 * LANES), BF16),
-        vmem((max(slots, new_count) * HALF, LANES), F32),
-        *[field] * 8,
+        vmem((slots * HALF, LANES), F32),
+        *[field] * 7,
         vmem((doms * code_rows, LANES), jnp.int16),
         vmem((doms * code_rows, LANES), jnp.int16),
         vmem((doms, LANES), F32),
         vmem((doms, LANES), F32),
         vmem((8 * HALF, LANES), F32),
-        vmem((8, LANES), F32),
-        vmem((steps, devices, LANES), F32),
+        vmem((steps, 2, LANES), F32),
+        vmem((steps, devices, 2, LANES), F32),
         dma((2,)), dma((2,)), dma((doms,)), dma((doms,)),
         dma((steps,)), dma((steps,)),
         dma((doms,)), dma((doms,)), dma((doms,)), dma((doms,)),
@@ -517,7 +538,7 @@
         send_index[0, 0].T, send_count[0], new_order[0], slot_target[0],
         state[0], cross_mass[0, 0], mass[0],
     )
-    return out[None]
+    return move(out)[None]
 
 
 def solution(mesh):

time: 53.2 us -> 72.6 us (1.36)
  Pallas kernels: 51 us -> 72.4 us
  local copies, waits for them, and re-layouts: 2.07 us -> 0 us
    pallas_call x0 -> x1, Pallas kernels: none -> 25 us  [move(): pl.pallas_call(move_kernel, out_shape=jax.ShapeDtypeStruct(value.shape, v...]
    pallas_call x1, Pallas kernels: 51 us -> 47.5 us  [per_device(): pl.pallas_call(functools.partial(kernel, slabs, doms, cap, group), out_sh...]
    unnamed x1 -> x0, local copies, waits for them, and re-layouts: 2.07 us -> none
where the time goes in v4:
time: 72.6 us; the launch traced here: 72.5 us
  Pallas kernels  72.4 us (100%)
    pallas_call x1, Pallas kernels, per_device(): pl.pallas_call(functools.partial(kernel, slabs, doms, cap, group), out_sh...  47.5 us
    pallas_call x1, Pallas kernels, move(): pl.pallas_call(move_kernel, out_shape=jax.ShapeDtypeStruct(value.shape, v...  25 us

profile of v4, /device:TPU:0, one launch (start us, length us, event | category | flops | bytes accessed | tf_op | source)
XLA Modules:
  0.0 72.5 jit_solution(3981400125170870363)
XLA Ops:
  0.0 47.5 %shard_map.73.src = f32[64,3072]{1,0:T(8,128)} custom-call(s32[4,16]{1,0:T(4,128)} %bitcast.13, s32[1,16]{1,0:T(1,128)} %bitcast.14, s32[1,64]{1,0:T(1,128)} %bitcast.15, s32[1,64]{1,0:T(1,128)} %bitcast.16, bf16[32,3072]{1,0:T(8,128)(2,1)} %bitcast.12, bf16[64,4096]{1,0:T(8,128)(2,1)} %bitcast.11, f32[64,4096]{1,0:T(8,128)} %bitcast.10), custom_call_target="tpu_custom_call" | custom-call | flops 1000000000 | bytes 4000000 | tf_op jit(solution)/shard_map/pallas_call | solution.py:526
  47.5 25.0 %shard_map.74 = f32[64,3072]{1,0:T(8,128)} custom-call(f32[64,3072]{1,0:T(8,128)} %shard_map.73.src), custom_call_target="tpu_custom_call" | custom-call | tf_op jit(solution)/shard_map/pallas_call | solution.py:478

commit v5 on v4

--- a/solution.py
+++ b/solution.py
@@ -194,7 +194,14 @@
         )
 
     def partner(i):
-        return lax.rem(my_dom + 1 + lax.rem(i + doms // 2 - 2, doms - 1), doms)
+        apart = lax.rem(i, 2) * (doms // 2) + lax.div(i, 2)
+        if doms & (doms - 1):
+            return lax.rem(my_dom + apart, doms)
+        other, bit = 0, 1
+        while bit < doms:
+            differ = lax.rem(lax.div(my_dom, bit) + lax.div(apart, bit), 2)
+            other, bit = other + differ * bit, bit * 2
+        return other
 
     def send_packet(i, carry):
         dom = partner(i)
@@ -460,18 +467,24 @@
         down.wait_send()
 
 
-def move_kernel(src, dst, sem):
+def move_kernel(src, dst, held, load_sem, store_sem):
     rows = src.shape[0] // 8
-    copies = [
-        pltpu.make_async_copy(
-            src.at[n * rows:(n + 1) * rows, :], dst.at[n * rows:(n + 1) * rows, :], sem.at[n]
-        )
-        for n in range(8)
+    parts = [slice(n * rows, (n + 1) * rows) for n in range(8)]
+    loads = [
+        pltpu.make_async_copy(src.at[part, :], held.at[part, :], load_sem.at[n])
+        for n, part in enumerate(parts)
     ]
-    for copy in copies:
-        copy.start()
-    for copy in copies:
-        copy.wait()
+    stores = [
+        pltpu.make_async_copy(held.at[part, :], dst.at[part, :], store_sem.at[n])
+        for n, part in enumerate(parts)
+    ]
+    for load in loads:
+        load.start()
+    for load, store in zip(loads, stores):
+        load.wait()
+        store.start()
+    for store in stores:
+        store.wait()
 
 
 def move(value):
@@ -480,7 +493,11 @@
         out_shape=jax.ShapeDtypeStruct(value.shape, value.dtype),
         in_specs=[pl.BlockSpec(memory_space=pl.ANY)],
         out_specs=pl.BlockSpec(memory_space=pl.ANY),
-        scratch_shapes=[pltpu.SemaphoreType.DMA((8,))],
+        scratch_shapes=[
+            pltpu.VMEM(value.shape, value.dtype),
+            pltpu.SemaphoreType.DMA((8,)),
+            pltpu.SemaphoreType.DMA((8,)),
+        ],
         compiler_params=pltpu.CompilerParams(vmem_limit_bytes=56 * 1024 * 1024),
     )(value)
 

time: 72.6 us -> 47.9 us (0.66)
  Pallas kernels: 72.4 us -> 47.7 us
    pallas_call x1, Pallas kernels: 25 us -> 1.99 us  [move(): pl.pallas_call(move_kernel, out_shape=jax.ShapeDtypeStruct(value.shape, v...]
    pallas_call x1, Pallas kernels: 47.5 us -> 45.7 us  [per_device(): pl.pallas_call(functools.partial(kernel, slabs, doms, cap, group), out_sh...]
where the time goes in v5:
time: 47.9 us; the launch traced here: 47.7 us
  Pallas kernels  47.7 us (100%)
    pallas_call x1, Pallas kernels, per_device(): pl.pallas_call(functools.partial(kernel, slabs, doms, cap, group), out_sh...  45.7 us
    pallas_call x1, Pallas kernels, move(): pl.pallas_call(move_kernel, out_shape=jax.ShapeDtypeStruct(value.shape, v...  1.99 us

profile of v5, /device:TPU:0, one launch (start us, length us, event | category | flops | bytes accessed | tf_op | source)
XLA Modules:
  0.0 47.7 jit_solution(3351266297152218361)
XLA Ops:
  0.0 45.7 %shard_map.73.src = f32[64,3072]{1,0:T(8,128)} custom-call(s32[4,16]{1,0:T(4,128)} %bitcast.13, s32[1,16]{1,0:T(1,128)} %bitcast.14, s32[1,64]{1,0:T(1,128)} %bitcast.15, s32[1,64]{1,0:T(1,128)} %bitcast.16, bf16[32,3072]{1,0:T(8,128)(2,1)} %bitcast.12, bf16[64,4096]{1,0:T(8,128)(2,1)} %bitcast.11, f32[64,4096]{1,0:T(8,128)} %bitcast.10), custom_call_target="tpu_custom_call" | custom-call | flops 1000000000 | bytes 4000000 | tf_op jit(solution)/shard_map/pallas_call | solution.py:543
  45.7 2.0 %shard_map.74 = f32[64,3072]{1,0:T(8,128)} custom-call(f32[64,3072]{1,0:T(8,128)} %shard_map.73.src), custom_call_target="tpu_custom_call" | custom-call | tf_op jit(solution)/shard_map/pallas_call | solution.py:491

commit v6 on v5

--- a/solution.py
+++ b/solution.py
@@ -74,26 +74,34 @@
 def kernel(
     slabs, doms, cap, group,
     index_ref, count_ref, order_ref, target_ref, state_hbm, cross_hbm, mass_hbm,
-    out_ref,
+    codes_out, scales_out,
     state_ref, cross_ref, mass_ref, load_sem,
     pool, up_out, down_out, up_in, down_in, packets, received, block, cross, blocks,
     contrib, residual, image, image2, image3, flat_x, flat_p, flat_r, codes, codes_in, scales, scales_in,
-    placed, sums, sums_in,
+    sums, sums_in,
     halo_send, halo_recv, packet_send, packet_recv, sum_send, sum_recv,
     code_send, code_recv, scale_send, scale_recv,
 ):
     my_slab, my_dom = lax.axis_index("slab"), lax.axis_index("dom")
     devices = slabs * doms
-    me = my_slab * doms + my_dom
     elements = state_ref.shape[0]
     slots = cross_ref.shape[0]
     new_count = mass_ref.shape[0]
     chunk = cap * HALF
     code_rows = codes.shape[0] // doms
 
-    def device(i):
-        there = lax.rem(me + i, devices)
-        return {"slab": lax.div(there, doms), "dom": lax.rem(there, doms)}
+    def wrap(value, size):
+        return jnp.where(value >= size, value - size, value)
+
+    def each_device(act):
+        for apart in range(slabs):
+            slab = wrap(my_slab + apart, slabs)
+
+            def body(i, carry, apart=apart, slab=slab):
+                act(apart * doms + i - 1, {"slab": slab, "dom": wrap(my_dom + i, doms)})
+                return carry
+
+            lax.fori_loop(1 if apart == 0 else 0, doms, body, 0, unroll=3 if apart == 0 else 4)
 
     loads = [
         pltpu.make_async_copy(src, dst, load_sem.at[n])
@@ -105,11 +113,10 @@
         load.start()
     barrier = pltpu.get_barrier_semaphore()
 
-    def greet(i, carry):
-        pl.semaphore_signal(barrier, inc=1, device_id=device(i), device_id_type=pl.DeviceIdType.MESH)
-        return carry
-
-    lax.fori_loop(1, devices, greet, 0)
+    def greet(i, where):
+        pl.semaphore_signal(barrier, inc=1, device_id=where, device_id_type=pl.DeviceIdType.MESH)
+
+    each_device(greet)
 
     loads[0].wait()
 
@@ -295,15 +302,14 @@
         own = jnp.concatenate([column_to_row(stack[:half]), column_to_row(stack[half:])], axis=0)
         sums[step] = own
 
-        def send(i, carry):
+        def send(i, where):
             pltpu.make_async_remote_copy(
-                src_ref=sums.at[step], dst_ref=sums_in.at[step, i - 1],
+                src_ref=sums.at[step], dst_ref=sums_in.at[step, i],
                 send_sem=sum_send.at[step], recv_sem=sum_recv.at[step],
-                device_id=device(i), device_id_type=pl.DeviceIdType.MESH,
+                device_id=where, device_id_type=pl.DeviceIdType.MESH,
             ).start()
-            return carry
-
-        lax.fori_loop(1, devices, send, 0)
+
+        each_device(send)
         return own
 
     def sum_end(step, own, count):
@@ -433,26 +439,22 @@
 
     lax.fori_loop(1, doms, send_code, 0)
     coded, scale = code(my_dom)
-    codes_in[pl.ds(at(my_dom, code_rows), code_rows), :] = coded
-    scales_in[pl.ds(my_dom, 1), :] = scale
-
-    def place(rows, carry):
-        for n in range(8 // group):
-            dom = rows * (8 // group) + n
-
-            @pl.when(dom != my_dom)
-            def _():
-                for copy in code_copies(dom, dom, dom):
-                    copy.wait()
-
-            value = codes_in[pl.ds(at(dom, code_rows), code_rows), :].astype(jnp.int32).astype(F32)[:used]
-            scale = row_to_column(scales_in[pl.ds(dom, 1), :], used)
-            placed[n * used:(n + 1) * used, :] = value * scale
-        for t in range(HALF):
-            out_ref[pl.ds(at(rows, 8), 8), t * LANES:(t + 1) * LANES] = placed[pl.ds(t, 8, stride=HALF), :]
-        return carry
-
-    lax.fori_loop(0, new_count // 8, place, 0)
+
+    codes_out[pl.ds(at(my_dom, code_rows), code_rows), :] = coded
+    scales_out[pl.ds(my_dom, 1), :] = scale
+
+    def take(dom, carry):
+        @pl.when(dom != my_dom)
+        def _():
+            for copy in code_copies(dom, dom, dom):
+                copy.wait()
+            here = pl.ds(at(dom, code_rows), code_rows)
+            codes_out[here, :] = codes_in[here, :]
+            scales_out[pl.ds(dom, 1), :] = scales_in[pl.ds(dom, 1), :]
+
+        return carry
+
+    lax.fori_loop(0, doms, take, 0)
 
     for step in range(SUMS):
         left = sums_in.at[step, 0:devices - 1]
@@ -467,39 +469,40 @@
         down.wait_send()
 
 
-def move_kernel(src, dst, held, load_sem, store_sem):
-    rows = src.shape[0] // 8
-    parts = [slice(n * rows, (n + 1) * rows) for n in range(8)]
-    loads = [
-        pltpu.make_async_copy(src.at[part, :], held.at[part, :], load_sem.at[n])
-        for n, part in enumerate(parts)
-    ]
-    stores = [
-        pltpu.make_async_copy(held.at[part, :], dst.at[part, :], store_sem.at[n])
-        for n, part in enumerate(parts)
-    ]
-    for load in loads:
-        load.start()
-    for load, store in zip(loads, stores):
-        load.wait()
+def unfold_kernel(used, code_rows, codes_ref, scales_ref, dst, placed, held, store_sem):
+    senders = 8 * HALF // used
+    stores = []
+    for block in range(held.shape[0] // 8):
+        for n in range(senders):
+            dom = block * senders + n
+            value = codes_ref[dom * code_rows:(dom + 1) * code_rows, :].astype(jnp.int32).astype(F32)[:used]
+            scale = row_to_column(scales_ref[dom:dom + 1, :], used)
+            row = (block * senders + n) * used
+            placed[row:row + used, :] = value * scale
+        part = slice(block * 8, (block + 1) * 8)
+        for t in range(HALF):
+            held[part, t * LANES:(t + 1) * LANES] = placed[pl.ds(block * 8 * HALF + t, 8, stride=HALF), :]
+        store = pltpu.make_async_copy(held.at[part, :], dst.at[part, :], store_sem.at[block])
         store.start()
+        stores.append(store)
     for store in stores:
         store.wait()
 
 
-def move(value):
+def unfold(codes, scales, new_count, used, code_rows):
+    shape = (new_count, V * Q)
     return pl.pallas_call(
-        move_kernel,
-        out_shape=jax.ShapeDtypeStruct(value.shape, value.dtype),
-        in_specs=[pl.BlockSpec(memory_space=pl.ANY)],
+        functools.partial(unfold_kernel, used, code_rows),
+        out_shape=jax.ShapeDtypeStruct(shape, F32),
+        in_specs=[pl.BlockSpec(memory_space=pltpu.VMEM)] * 2,
         out_specs=pl.BlockSpec(memory_space=pl.ANY),
         scratch_shapes=[
-            pltpu.VMEM(value.shape, value.dtype),
-            pltpu.SemaphoreType.DMA((8,)),
-            pltpu.SemaphoreType.DMA((8,)),
+            pltpu.VMEM((new_count * HALF, LANES), F32),
+            pltpu.VMEM(shape, F32),
+            pltpu.SemaphoreType.DMA((new_count // 8,)),
         ],
         compiler_params=pltpu.CompilerParams(vmem_limit_bytes=56 * 1024 * 1024),
-    )(value)
+    )(codes, scales)
 
 
 def per_device(slabs, doms, state, send_index, send_count, slot_target, cross_mass, mass, new_order):
@@ -533,19 +536,21 @@
         vmem((doms * code_rows, LANES), jnp.int16),
         vmem((doms, LANES), F32),
         vmem((doms, LANES), F32),
-        vmem((8 * HALF, LANES), F32),
         vmem((steps, 2, LANES), F32),
         vmem((steps, devices, 2, LANES), F32),
         dma((2,)), dma((2,)), dma((doms,)), dma((doms,)),
         dma((steps,)), dma((steps,)),
         dma((doms,)), dma((doms,)), dma((doms,)), dma((doms,)),
     ]
-    out = pl.pallas_call(
+    codes, scales = pl.pallas_call(
         functools.partial(kernel, slabs, doms, cap, group),
-        out_shape=jax.ShapeDtypeStruct((new_count, V * Q), F32),
+        out_shape=(
+            jax.ShapeDtypeStruct((doms * code_rows, LANES), jnp.int16),
+            jax.ShapeDtypeStruct((doms, LANES), F32),
+        ),
         in_specs=[pl.BlockSpec(memory_space=smem)] * 3 + [pl.BlockSpec(memory_space=vmem)]
         + [pl.BlockSpec(memory_space=pltpu.HBM)] * 3,
-        out_specs=pl.BlockSpec(memory_space=vmem),
+        out_specs=[pl.BlockSpec(memory_space=vmem)] * 2,
         scratch_shapes=scratch,
         compiler_params=pltpu.CompilerParams(
             collective_id=0, has_side_effects=True, vmem_limit_bytes=56 * 1024 * 1024
@@ -555,7 +560,7 @@
         send_index[0, 0].T, send_count[0], new_order[0], slot_target[0],
         state[0], cross_mass[0, 0], mass[0],
     )
-    return move(out)[None]
+    return unfold(codes, scales, new_count, group * HALF, code_rows)[None]
 
 
 def solution(mesh):

time: 47.9 us -> 47.5 us (level)
  no operation moved by 1% of the time
where the time goes in v6:
time: 47.5 us; the launch traced here: 47.3 us
  Pallas kernels  47.3 us (100%)
    pallas_call x1, Pallas kernels, per_device(): pl.pallas_call(functools.partial(kernel, slabs, doms, cap, group), out_sh...  45.3 us
    pallas_call x1, Pallas kernels, unfold(): pl.pallas_call(functools.partial(unfold_kernel, used, code_rows), out_sha...  2.06 us

profile of v6, /device:TPU:0, one launch (start us, length us, event | category | flops | bytes accessed | tf_op | source)
XLA Modules:
  0.0 47.3 jit_solution(8902175482112034928)
XLA Ops:
  0.0 45.3 %shard_map.73 = (s16[1536,128]{1,0:T(8,128)(2,1)}, f32[16,128]{1,0:T(8,128)}) custom-call(s32[4,16]{1,0:T(4,128)} %bitcast.13, s32[1,16]{1,0:T(1,128)} %bitcast.14, s32[1,64]{1,0:T(1,128)} %bitcast.15, s32[1,64]{1,0:T(1,128)} %bitcast.16, bf16[32,3072]{1,0:T(8,128)(2,1)} %bitcast.12, bf16[64,4096]{1,0:T(8,128)(2,1)} %bitcast.11, f32[64,4096]{1,0:T(8,128)} %bitcast.10), custom_call_target="tpu_custom_call" | custom-call | flops 1000000000 | bytes 4000000 | tf_op jit(solution)/shard_map/pallas_call | solution.py:545
  45.3 2.1 %shard_map.74 = f32[64,3072]{1,0:T(8,128)} custom-call(s16[1536,128]{1,0:T(8,128)(2,1)} %get-tuple-element.7.codes_ref, f32[16,128]{1,0:T(8,128)} %get-tuple-element.8.scales_ref), custom_call_target="tpu_custom_call" | custom-call | tf_op jit(solution)/shard_map/pallas_call | solution.py:494

commit v7 on v6

--- a/solution.py
+++ b/solution.py
@@ -247,8 +247,6 @@
 
         return carry
 
-    lax.fori_loop(0, doms, arrive, 0)
-
     senders = 16 // cap
 
     def product(step, carry):
@@ -265,7 +263,10 @@
             )
         return carry
 
-    lax.fori_loop(0, doms // 2, product, 0, unroll=4)
+    own_half = jnp.where(my_dom >= doms // 2, 1, 0)
+    for half in (own_half, 1 - own_half):
+        lax.fori_loop(0, doms // 2, lambda n, c, half=half: arrive(half * (doms // 2) + n, c), 0)
+        lax.fori_loop(0, doms // 4, lambda n, c, half=half: product(half * (doms // 4) + n, c), 0, unroll=4)
 
     shape = (new_count, slots)
     onehot = jnp.where(lax.broadcasted_iota(jnp.int32, shape, 0) == target_ref[...], 1.0, 0.0).astype(BF16)

time: 47.5 us -> 47.1 us (level)
  no operation moved by 1% of the time
where the time goes in v7:
time: 47.1 us; the launch traced here: 46.9 us
  Pallas kernels  46.9 us (100%)
    pallas_call x1, Pallas kernels, per_device(): pl.pallas_call(functools.partial(kernel, slabs, doms, cap, group), out_sh...  44.9 us
    pallas_call x1, Pallas kernels, unfold(): pl.pallas_call(functools.partial(unfold_kernel, used, code_rows), out_sha...  2.06 us

profile of v7, /device:TPU:0, one launch (start us, length us, event | category | flops | bytes accessed | tf_op | source)
XLA Modules:
  0.0 46.9 jit_solution(2500266609524139037)
XLA Ops:
  0.0 44.9 %shard_map.73 = (s16[1536,128]{1,0:T(8,128)(2,1)}, f32[16,128]{1,0:T(8,128)}) custom-call(s32[4,16]{1,0:T(4,128)} %bitcast.13, s32[1,16]{1,0:T(1,128)} %bitcast.14, s32[1,64]{1,0:T(1,128)} %bitcast.15, s32[1,64]{1,0:T(1,128)} %bitcast.16, bf16[32,3072]{1,0:T(8,128)(2,1)} %bitcast.12, bf16[64,4096]{1,0:T(8,128)(2,1)} %bitcast.11, f32[64,4096]{1,0:T(8,128)} %bitcast.10), custom_call_target="tpu_custom_call" | custom-call | flops 1000000000 | bytes 4000000 | tf_op jit(solution)/shard_map/pallas_call | solution.py:546
  44.9 2.1 %shard_map.74 = f32[64,3072]{1,0:T(8,128)} custom-call(s16[1536,128]{1,0:T(8,128)(2,1)} %get-tuple-element.7.codes_ref, f32[16,128]{1,0:T(8,128)} %get-tuple-element.8.scales_ref), custom_call_target="tpu_custom_call" | custom-call | tf_op jit(solution)/shard_map/pallas_call | solution.py:495

commit v8 on v7

--- a/solution.py
+++ b/solution.py
@@ -216,7 +216,7 @@
         packet(dom).start()
         return carry
 
-    lax.fori_loop(1, doms, send_packet, 0)
+    lax.fori_loop(1, doms, send_packet, 0, unroll=3)
     received[pl.ds(at(my_dom, chunk), chunk), :] = pick(my_dom)
 
     lax.fori_loop(new_count // 32, new_count // 16, prepare_mass, 0)
@@ -334,7 +334,7 @@
         image2[at_pair, :] = q
         return bb + b * b, bw + b * w, ww + w * w, wq + w * q
 
-    own = sum_start(0, lax.fori_loop(0, pairs, first_pass, (zero,) * 4, unroll=8))
+    own = sum_start(0, lax.fori_loop(0, pairs, first_pass, (zero,) * 4, unroll=16))
 
     def third_image(pair, carry):
         at_pair = pl.ds(at(pair, V), V)
@@ -438,7 +438,7 @@
             copy.start()
         return carry
 
-    lax.fori_loop(1, doms, send_code, 0)
+    lax.fori_loop(1, doms, send_code, 0, unroll=3)
     coded, scale = code(my_dom)
 
     codes_out[pl.ds(at(my_dom, code_rows), code_rows), :] = coded

time: 47.1 us -> 46.6 us (0.989)
  Pallas kernels: 46.9 us -> 46.4 us
    pallas_call x1, Pallas kernels: 44.9 us -> 44.4 us  [per_device(): pl.pallas_call(functools.partial(kernel, slabs, doms, cap, group), out_sh...]
where the time goes in v8:
time: 46.6 us; the launch traced here: 46.4 us
  Pallas kernels  46.4 us (100%)
    pallas_call x1, Pallas kernels, per_device(): pl.pallas_call(functools.partial(kernel, slabs, doms, cap, group), out_sh...  44.4 us
    pallas_call x1, Pallas kernels, unfold(): pl.pallas_call(functools.partial(unfold_kernel, used, code_rows), out_sha...  2.06 us

profile of v8, /device:TPU:0, one launch (start us, length us, event | category | flops | bytes accessed | tf_op | source)
XLA Modules:
  0.0 46.4 jit_solution(556705515657759036)
XLA Ops:
  0.0 44.4 %shard_map.73 = (s16[1536,128]{1,0:T(8,128)(2,1)}, f32[16,128]{1,0:T(8,128)}) custom-call(s32[4,16]{1,0:T(4,128)} %bitcast.13, s32[1,16]{1,0:T(1,128)} %bitcast.14, s32[1,64]{1,0:T(1,128)} %bitcast.15, s32[1,64]{1,0:T(1,128)} %bitcast.16, bf16[32,3072]{1,0:T(8,128)(2,1)} %bitcast.12, bf16[64,4096]{1,0:T(8,128)(2,1)} %bitcast.11, f32[64,4096]{1,0:T(8,128)} %bitcast.10), custom_call_target="tpu_custom_call" | custom-call | flops 1000000000 | bytes 4000000 | tf_op jit(solution)/shard_map/pallas_call | solution.py:546
  44.4 2.1 %shard_map.74 = f32[64,3072]{1,0:T(8,128)} custom-call(s16[1536,128]{1,0:T(8,128)(2,1)} %get-tuple-element.7.codes_ref, f32[16,128]{1,0:T(8,128)} %get-tuple-element.8.scales_ref), custom_call_target="tpu_custom_call" | custom-call | tf_op jit(solution)/shard_map/pallas_call | solution.py:495
